TPU v7x, 32 devices: a whole 2x2x4 slice. The times are simulated.
32 devices in a mesh: dp: 16 (over z, y, core), tensor: 2 (over x).
Axes of the slice: x: 2, y: 2, z: 4, core: 2. Of those that a mesh axis runs over, the one named last changes fastest.
Arguments:
- inputs: bfloat16 [16, 512, 1024], P('dp', 'tensor'), may hold values from -6 to 6
- segments: int32 [16, 512], P('dp'), may hold values from 0 to 2, as said below
- w_query: bfloat16 [1024, 1024], P('dp', 'tensor'), may hold values from -0.1875 to 0.1875
- w_key: bfloat16 [1024, 1024], P('dp', 'tensor'), may hold values from -0.1875 to 0.1875
- w_value: bfloat16 [1024, 1024], P('dp', 'tensor'), may hold values from -0.1875 to 0.1875
- w_output: bfloat16 [1024, 1024], P('tensor', 'dp'), may hold values from -3 to 3
- w_expand: bfloat16 [1024, 4096], P('dp', 'tensor'), may hold values from -0.1875 to 0.1875
- w_reduce: bfloat16 [4096, 1024], P('tensor', 'dp'), may hold values from -0.09375 to 0.09375
- query_bias_vector: float32 [1024], P('tensor'), may hold values from -3 to 3
- b_value: float32 [1024], P('tensor'), may hold values from -3 to 3
- b_output: float32 [1024], replicated, may hold values from -3 to 3
- b_expand: float32 [4096], P('tensor'), may hold values from -3 to 3
- b_reduce: float32 [1024], replicated, may hold values from -3 to 3
- gain_first: float32 [1024], replicated, may hold values from 0.5 to 1.5
- shift_first: float32 [1024], replicated, may hold values from -3 to 3
- gain_second: float32 [1024], replicated, may hold values from 0.5 to 1.5
- shift_second: float32 [1024], replicated, may hold values from -3 to 3
- cotangent: bfloat16 [16, 512, 1024], P('dp', 'tensor'), may hold values from -6 to 6
Outputs:
- result: bfloat16 [16, 512, 1024], P('dp', 'tensor')
- grad_inputs: float32 [16, 512, 1024], P('dp', 'tensor')
- grad_w_query: float32 [1024, 1024], P('dp', 'tensor')
- key_weight_gradient: float32 [1024, 1024], P('dp', 'tensor')
- grad_w_value: float32 [1024, 1024], P('dp', 'tensor')
- grad_w_output: float32 [1024, 1024], P('tensor', 'dp')
- grad_w_expand: float32 [1024, 4096], P('dp', 'tensor')
- grad_w_reduce: float32 [4096, 1024], P('tensor', 'dp')
- grad_b_query: float32 [1024], P('tensor')
- grad_b_value: float32 [1024], P('tensor')
- grad_b_output: float32 [1024], replicated
- grad_b_expand: float32 [4096], P('tensor')
- grad_b_reduce: float32 [1024], replicated
- grad_gain_first: float32 [1024], replicated
- grad_shift_first: float32 [1024], replicated
- grad_gain_second: float32 [1024], replicated
- grad_shift_second: float32 [1024], replicated
Inputs may be any that keep to these rules, and one draw needn't show every extreme that they name: `segments`: segment numbers never fall along a sequence; equal numbers mark tokens of one document. Of the 1 sequence of each index of dp, one holds a single document.
All inputs are finite; a program needn't handle non-finite values.
Results may differ from a plain program's by a relative error of at most 0.018.
Values may be sent and summed in bfloat16 or wider, within the bound.
No kernel may reach another device: no remote copies, remote signals or barrier semaphores. Data moves between devices by JAX's collectives and lax.ppermute only.
A program may use at most 128 MiB of HBM per device.

v0:
```python
import functools

import jax
import jax.numpy as jnp
from jax import lax
from jax.experimental import pallas as pl
from jax.experimental.pallas import tpu as pltpu
from jax.sharding import PartitionSpec as P

HD = 64
NORM_EPS = 1e-05
MASKED = -1e30
BF = jnp.bfloat16
F32 = jnp.float32
PARAMS = pltpu.CompilerParams(vmem_limit_bytes=60 << 20)
VMEM = pl.BlockSpec(memory_space=pltpu.VMEM)
SMEM = pl.BlockSpec(memory_space=pltpu.SMEM)
ANY = pl.BlockSpec(memory_space=pltpu.HBM)


def dot(a, b):
    return lax.dot_general(a, b, (((1,), (0,)), ((), ())), preferred_element_type=F32)


def dot_nt(a, b):
    return lax.dot_general(a, b, (((1,), (1,)), ((), ())), preferred_element_type=F32)


def dot_tn(a, b):
    return lax.dot_general(a, b, (((0,), (0,)), ((), ())), preferred_element_type=F32)


def cost(flops, nbytes):
    return pl.CostEstimate(flops=flops // 1024, bytes_accessed=nbytes // 1024, transcendentals=0)


def lane_half(array, head):
    lanes = lax.broadcasted_iota(jnp.int32, array.shape, 1)
    return jnp.where((lanes < HD) == (head == 0), array, jnp.zeros_like(array))


def column_of(row):
    return jnp.broadcast_to(row, (128, row.shape[1])).T[:, :1]


def attend_forward_kernel(parts, qkv_ref, row_ref, out_w_ref, *refs):
    ctx_ref, lse_ref, part_refs, scratch = refs[0], refs[1], refs[2 : 2 + parts], refs[-1]
    query, key, value = (qkv_ref[:, i * 128 : (i + 1) * 128] for i in range(3))
    same = column_of(row_ref[0]) == row_ref[0]
    query = query * jnp.asarray(HD**-0.5, BF)
    value_t = value.T
    out = []
    for head in range(2):
        scores = dot_nt(key, lane_half(query, head))
        scores = jnp.where(same, scores, MASKED)
        top = jnp.max(scores, axis=0, keepdims=True)
        weights = jnp.exp(scores - top)
        total = jnp.sum(weights, axis=0, keepdims=True)
        probs = (weights * (1.0 / total)).astype(BF)
        lse_ref[0, head : head + 1, :] = top + jnp.log(total)
        out.append(dot(value_t[head * HD : (head + 1) * HD], probs))
    context = jnp.concatenate(out, axis=0).T.astype(BF)
    ctx_ref[...] = context
    pair, pairs = pl.program_id(1), pl.num_programs(1)
    scratch[pair] = context

    @pl.when(pair == pairs - 1)
    def _():
        span = part_refs[0].shape[0]
        whole = jnp.concatenate([scratch[i] for i in range(scratch.shape[0])], axis=1)
        for j, part_ref in enumerate(part_refs):
            part_ref[...] = dot_nt(whole[j * span : (j + 1) * span], out_w_ref[...]).astype(BF)


def attend_forward(qkv, rows, full_attn, parts):
    seqs, _, length = rows.shape
    pairs = qkv.shape[1] // 384
    local, width, span = 128 * pairs, full_attn.shape[0], length // parts
    out = pl.pallas_call(
        functools.partial(attend_forward_kernel, parts),
        grid=(seqs, pairs),
        in_specs=[
            pl.BlockSpec((length, 384), lambda s, p: (s, p)),
            pl.BlockSpec((1, 1, length), lambda s, p: (s, 0, 0)),
            pl.BlockSpec((width, local), lambda s, p: (0, 3)),
        ],
        out_specs=[
            pl.BlockSpec((length, 128), lambda s, p: (s, p)),
            pl.BlockSpec((1, 2, length), lambda s, p: (s * pairs + p, 0, 0)),
        ]
        + [pl.BlockSpec((span, width), lambda s, p: (s, 0))] * parts,
        out_shape=[
            jax.ShapeDtypeStruct((seqs * length, local), BF),
            jax.ShapeDtypeStruct((seqs * pairs, 2, length), F32),
        ]
        + [jax.ShapeDtypeStruct((seqs * span, width), BF)] * parts,
        scratch_shapes=[pltpu.VMEM((pairs, length, 128), BF)],
        compiler_params=PARAMS,
        cost_estimate=cost(seqs * pairs * 24 * 128 * length * length, 8 << 20),
    )(qkv, rows, full_attn)
    return out[0], out[1], out[2:]


def attend_backward_body(qkv_ref, row_ref, lse_ref, w_ref, parts, *refs):
    out_ref, sum_ref = refs[parts : parts + 2]
    query, key, value = (qkv_ref[:, i * 128 : (i + 1) * 128] for i in range(3))
    grad_ctx = jnp.concatenate([ref[...] for ref in refs[:parts]], axis=0)
    same = column_of(row_ref[0]) == row_ref[0]
    small_query = query * jnp.asarray(HD**-0.5, BF)
    key_t = key.T
    grad_q, grad_k, grad_v = [], [], []
    for head in range(2):
        scores = dot_nt(key, lane_half(small_query, head))
        probs = jnp.exp(jnp.where(same, scores, MASKED) - lse_ref[0, head : head + 1, :])
        grad_probs = dot_nt(value, lane_half(grad_ctx, head))
        inner = jnp.sum(probs * grad_probs, axis=0, keepdims=True)
        grad_scores = (probs * (grad_probs - inner)).astype(BF)
        grad_q.append(dot(key_t[head * HD : (head + 1) * HD], grad_scores))
        grad_k.append(dot(grad_scores, query))
        grad_v.append(dot(probs.astype(BF), grad_ctx))
    lanes = lax.broadcasted_iota(jnp.int32, grad_k[0].shape, 1) < HD
    factor = HD**-0.5
    outs = (
        jnp.concatenate(grad_q, axis=0).T * factor,
        jnp.where(lanes, grad_k[0], grad_k[1]) * factor,
        jnp.where(lanes, grad_v[0], grad_v[1]),
    )
    for i, value in enumerate(outs):
        low = value.astype(BF)
        out_ref[:, i * 128 : (i + 1) * 128] = low
        sum_ref[0, :, i * 128 : (i + 1) * 128] = jnp.sum(
            low.astype(F32), axis=0, keepdims=True
        )


def attend_backward_kernel(parts, halved, me_ref, qkv_ref, row_ref, lse_ref, w_ref, *refs):
    attend_backward_body(qkv_ref, row_ref, lse_ref, w_ref, parts, *refs)
    out_ref, back_refs, total = refs[parts], refs[parts + 2 : 2 * parts + 2], refs[-1]
    pair, pairs = pl.program_id(1), pl.num_programs(1)
    part = dot_nt(out_ref[...], w_ref[...])

    @pl.when(pair == 0)
    def _():
        total[...] = part

    @pl.when(pair != 0)
    def _():
        total[...] += part

    @pl.when(pair == pairs - 1)
    def _():
        span = back_refs[0].shape[0]
        for j, ref in enumerate(back_refs):
            ref[...] = total[j * span : (j + 1) * span, :].astype(ref.dtype)

    if halved:
        give_ref = refs[2 * parts + 2]

        @pl.when(pair // (pairs // 2) == 1 - me_ref[0] % 2)
        def _():
            give_ref[...] = out_ref[...]


def attend_backward(me, qkv, rows, lse, full_attn, grad_ctx):
    seqs, _, length = rows.shape
    pairs = qkv.shape[1] // 384
    half = pairs // 2
    parts = len(grad_ctx)
    span, width = length // parts, full_attn.shape[0]
    kernel = functools.partial(attend_backward_kernel, parts, half > 0)

    def give_place(s, p, m):
        return s, jnp.clip(p - half * (1 - m[0] % 2), 0, max(half - 1, 0))

    out = pl.pallas_call(
        kernel,
        grid_spec=pltpu.PrefetchScalarGridSpec(
            num_scalar_prefetch=1,
            grid=(seqs, pairs),
            in_specs=[
                pl.BlockSpec((length, 384), lambda s, p, m: (s, p)),
                pl.BlockSpec((1, 1, length), lambda s, p, m: (s, 0, 0)),
                pl.BlockSpec((1, 2, length), lambda s, p, m: (s * pairs + p, 0, 0)),
                pl.BlockSpec((width, 384), lambda s, p, m: (0, p)),
            ]
            + [
                pl.BlockSpec((length // len(grad_ctx), 128), lambda s, p, m: (s, p))
                for _ in grad_ctx
            ],
            out_specs=[
                pl.BlockSpec((length, 384), lambda s, p, m: (s, p)),
                pl.BlockSpec((1, 1, 384), lambda s, p, m: (s, 0, p)),
            ]
            + [pl.BlockSpec((span, width), lambda s, p, m: (s, 0))] * parts
            + ([pl.BlockSpec((length, 384), give_place)] if half else []),
            scratch_shapes=[pltpu.VMEM((length, width), F32)],
        ),
        out_shape=[
            jax.ShapeDtypeStruct(qkv.shape, BF),
            jax.ShapeDtypeStruct((seqs, 1, qkv.shape[1]), F32),
        ]
        + [jax.ShapeDtypeStruct((seqs * span, width), BF if j else F32) for j in range(parts)]
        + ([jax.ShapeDtypeStruct((qkv.shape[0], 384 * half), BF)] if half else []),
        compiler_params=PARAMS,
        cost_estimate=cost(seqs * pairs * 40 * 128 * length * length, 8 << 20),
    )(me, qkv, rows, lse, full_attn, *grad_ctx)
    bias = jnp.sum(out[1], axis=(0, 1))
    return out[0], bias, out[-1] if half else None, list(out[2 : 2 + parts])


def ring_chip(place, chips):
    return jnp.where(place < chips // 2, 2 * place, 2 * (chips - 1 - place) + 1)


def ring_place(chip, chips):
    return jnp.where(chip % 2 == 0, chip // 2, chips - 1 - chip // 2)


def chip_at(me, distance, chips):
    return ring_chip((ring_place(me // 2, chips) + distance + chips) % chips, chips)


def gathered_rows(me, plan, rows, chips):
    out = []
    for distance, other, row in plan:
        core = me % 2
        owner = 2 * chip_at(me, distance, chips) + (1 - core if other else core)
        out.append(pl.multiple_of(owner * rows + row, 16))
    return out


def place_pieces(me, plan, rows, chips, pieces, out, sem):
    copies = [
        pltpu.make_async_copy(piece, out.at[pl.ds(row, piece.shape[0]), :], sem.at[i])
        for i, (piece, row) in enumerate(
            zip(pieces, gathered_rows(me, plan, rows, chips))
        )
    ]
    for copy in copies:
        copy.start()
    for copy in copies:
        copy.wait()


def assemble_kernel(plan, rows, chips, me_ref, *refs):
    pieces, out, sem = refs[: len(plan)], refs[-2], refs[-1]
    place_pieces(me_ref[0], plan, rows, chips, pieces, out, sem)


def assemble(me, plan, pieces, rows, chips):
    cols = pieces[0].shape[1]
    return pl.pallas_call(
        functools.partial(assemble_kernel, plan, rows, chips),
        out_shape=jax.ShapeDtypeStruct((2 * chips * rows, cols), BF),
        in_specs=[SMEM] + [ANY] * len(plan),
        out_specs=VMEM,
        scratch_shapes=[pltpu.SemaphoreType.DMA((len(plan),))],
        compiler_params=PARAMS,
        cost_estimate=cost(0, 8 * chips * rows * cols),
    )(me, *pieces)


def project_kernel(plan, rows, chips, parts, me_ref, bias_ref, *refs):
    blocks, pieces = refs[:parts], refs[parts : parts + len(plan)]
    full_out, out, full, sem, out_sem = refs[parts + len(plan) :]
    place_pieces(me_ref[0], plan, rows, chips, pieces, full, sem)
    copy = pltpu.make_async_copy(full, full_out, out_sem)
    copy.start()
    cols = out.shape[1]
    count = blocks[0].shape[0]
    for i, block in enumerate(blocks):
        for start in range(0, cols, 384):
            out[i * count : (i + 1) * count, start : start + 384] = (
                dot(block[...], full[:, start : start + 384])
                + bias_ref[:, start : start + 384]
            ).astype(BF)
    copy.wait()


def project(me, plan, pieces, rows, chips, blocks, bias):
    cols, wide = pieces[0].shape[1], bias.shape[1]
    count, width = blocks[0].shape
    tokens = count * len(blocks)
    return pl.pallas_call(
        functools.partial(project_kernel, plan, rows, chips, len(blocks)),
        out_shape=[
            jax.ShapeDtypeStruct((width, cols), BF),
            jax.ShapeDtypeStruct((tokens, wide), BF),
        ],
        in_specs=[SMEM, VMEM] + [VMEM] * len(blocks) + [ANY] * len(plan),
        out_specs=[ANY, VMEM],
        scratch_shapes=[
            pltpu.VMEM((width, cols), BF),
            pltpu.SemaphoreType.DMA((len(plan),)),
            pltpu.SemaphoreType.DMA,
        ],
        compiler_params=PARAMS,
        cost_estimate=cost(2 * tokens * width * wide, 8 * width * cols),
    )(me, bias, *blocks, *pieces)


def grad_kernel(chips, sources, terms, me_ref, *refs):
    scratch, out = refs[-1], refs[-2]
    d = 2 * pl.program_id(0)
    rows = out.shape[1]
    k = 0
    for col, term in zip(terms, sources):
        total = None
        for _ in range(term):
            pair = jnp.concatenate([refs[k][...], refs[k + 1][...]], axis=1)
            product = dot_tn(pair, refs[k + 2][...])
            total = product if total is None else total + product
            k += 3
        cols = slice(col, col + total.shape[1])
        if total.shape[0] == 2 * rows:
            out[0, :, cols] = total[:rows].astype(BF)
            out[1, :, cols] = total[rows:].astype(BF)
        else:
            lanes = total.shape[0] // 2
            scratch[:, cols] = total
            for i in range(2):
                off = lanes * i + (chip_at(me_ref[0], d + i, chips) * rows) % lanes
                out[i, :, cols] = scratch[pl.ds(pl.multiple_of(off, 32), rows), cols].astype(BF)


def pair_grads(me, chips, terms):
    width = terms[0][0][0].shape[1]
    rows = width // chips
    lanes = max(rows, 128)
    specs, arrays, cols, sources, start, flops = [], [], [], [], 0, 0
    for term in terms:
        cols.append(start)
        sources.append(len(term))
        for wide, narrow, both, row in term:
            count, most = wide.shape[0], narrow.shape[1]
            half = most // 2 if both else most
            if both and half % 128:
                narrow = lax.dynamic_slice_in_dim(narrow, half * (me[0] % 2), half, 1)
                both = False
            specs += [
                pl.BlockSpec(
                    (count, lanes),
                    lambda d, m, i=i: (0, chip_at(m[0], 2 * d + i, chips) * rows // lanes),
                )
                for i in range(2)
            ] + [
                pl.BlockSpec(
                    (count, half),
                    lambda d, m, both=both, row=row: (row, m[0] % 2 if both else 0),
                ),
            ]
            arrays += [wide, wide, narrow]
            flops += 2 * count * width * half
        start += half
    return pl.pallas_call(
        functools.partial(grad_kernel, chips, sources, cols),
        grid_spec=pltpu.PrefetchScalarGridSpec(
            num_scalar_prefetch=1,
            grid=(chips // 2,),
            in_specs=specs,
            out_specs=pl.BlockSpec((2, rows, start), lambda d, m: (d, 0, 0)),
            scratch_shapes=[pltpu.VMEM((2 * lanes, start if lanes > rows else 128), F32)],
        ),
        out_shape=jax.ShapeDtypeStruct((chips, rows, start), BF),
        compiler_params=PARAMS,
        cost_estimate=cost(flops, 8 << 20),
    )(me, *arrays)


def start_all(pairs, sem):
    copies = [
        pltpu.make_async_copy(source, target, sem.at[i])
        for i, (source, target) in enumerate(pairs)
    ]
    for copy in copies:
        copy.start()
    return copies


def wait_all(copies):
    for copy in copies:
        copy.wait()


def start_weights(me, plan, rows, chips, sources, which, out, sem):
    wide = out.shape[1]
    if plan is None:
        half = wide // 2
        return [
            start_all(
                [(sources[which].at[:, k : k + half], out.at[:, k : k + half])],
                sem.at[pl.ds(k // half, 1)],
            )
            for k in (0, half)
        ]
    return [
        start_all(
            [
                (
                    piece.at[:, which * wide : (which + 1) * wide],
                    out.at[pl.ds(row, piece.shape[0]), :],
                )
                for piece, row in zip(sources, gathered_rows(me, plan, rows, chips))
            ],
            sem,
        )
    ]


def halves(me, kept, own, give):
    wide = own.shape[1]
    core = me % 2
    return [
        (kept.at[:, pl.ds(pl.multiple_of(wide * core, 128), wide)], own),
        (kept.at[:, pl.ds(pl.multiple_of(wide * (1 - core), 128), wide)], give),
    ]


def ffn_forward_kernel(plan, rows, chips, me_ref, bias_o, gain, shift, bias_e, *refs):
    count = 2 if plan is None else len(plan)
    ins, pieces, refs = refs[:3], refs[3 : 3 + count], refs[3 + count :]
    unit_out, low_out, own_out, give_out, slope_out = refs[:5]
    kept_out, refs = ((), refs) if plan is None else (refs[5:7], refs[2:])
    scale_out, part_out, refs = refs[5], refs[6], refs[7:]
    (
        tok, own, got, expand, reduce, unit_keep, low_keep, act_keep, slope_keep,
        sem, expand_sem, reduce_sem, out_sem,
    ) = refs
    me = me_ref[0]
    hidden = act_keep.shape[1]
    loads = start_all(zip(ins, (tok, own, got)), sem)
    expand_loads = start_weights(me, plan, rows, chips, pieces, 0, expand, expand_sem)
    reduce_loads = start_weights(me, plan, rows, chips, pieces, 1, reduce, reduce_sem)
    wait_all(loads)
    normed, unit, scale = ln_forward(
        tok[...].astype(F32) + (own[...].astype(F32) + got[...].astype(F32)) + bias_o[...],
        gain[...],
        shift[...],
    )
    scale_out[...] = scale
    unit_keep[...] = unit
    low_keep[...] = normed.astype(BF)
    copies = start_all([(unit_keep, unit_out), (low_keep, low_out)], out_sem)
    parts = len(expand_loads)
    step = min(512, hidden // parts)
    for start in range(0, hidden, step):
        if start % (hidden // parts) == 0:
            wait_all(expand_loads[start * parts // hidden])
        cols = slice(start, start + step)
        act, slope = gelu_pair(dot(low_keep[...], expand[:, cols]) + bias_e[:, cols])
        act_keep[:, cols] = act.astype(BF)
        slope_keep[:, cols] = slope.astype(BF)
    copies += start_all(
        halves(me, act_keep, own_out, give_out) + [(slope_keep, slope_out)],
        out_sem.at[pl.ds(2, 3)],
    )
    for load in reduce_loads:
        wait_all(load)
    if kept_out:
        copies += start_all(
            zip((expand, reduce), kept_out), out_sem.at[pl.ds(5, 2)]
        )
    part_out[...] = dot_nt(act_keep[...], reduce[...]).astype(BF)
    wait_all(copies)


def ffn_weights(ring, weights):
    if weights is None:
        return ring.plan, ring.pieces
    return None, weights


def ffn_scratch(sources, width, hidden):
    pieces = len(sources)
    return [pltpu.VMEM((width, hidden), BF)] * 2, [
        pltpu.SemaphoreType.DMA((pieces,)),
        pltpu.SemaphoreType.DMA((pieces,)),
    ]


def ffn_forward(me, ring, weights, chips, tok, own, got, bias_o, gain, shift, bias_e):
    count, width = tok.shape
    hidden = bias_e.shape[0]
    plan, sources = ffn_weights(ring, weights)
    scratch, sems = ffn_scratch(sources, width, hidden)
    kept = [] if weights else [jax.ShapeDtypeStruct((width, hidden), BF)] * 2
    out = pl.pallas_call(
        functools.partial(ffn_forward_kernel, plan, ring.rows, chips),
        out_shape=[
            jax.ShapeDtypeStruct((count, width), F32),
            jax.ShapeDtypeStruct((count, width), BF),
            jax.ShapeDtypeStruct((count, hidden // 2), BF),
            jax.ShapeDtypeStruct((count, hidden // 2), BF),
            jax.ShapeDtypeStruct((count, hidden), BF),
        ]
        + kept
        + [
            jax.ShapeDtypeStruct((count, 1), F32),
            jax.ShapeDtypeStruct((count, width), BF),
        ],
        in_specs=[SMEM] + [VMEM] * 4 + [ANY] * (3 + len(sources)),
        out_specs=[ANY] * (5 + len(kept)) + [VMEM] * 2,
        scratch_shapes=[pltpu.VMEM((count, width), BF)] * 3
        + scratch
        + [
            pltpu.VMEM((count, width), F32),
            pltpu.VMEM((count, width), BF),
            pltpu.VMEM((count, hidden), BF),
            pltpu.VMEM((count, hidden), BF),
            pltpu.SemaphoreType.DMA((3,)),
        ]
        + sems
        + [pltpu.SemaphoreType.DMA((5 + len(kept),))],
        compiler_params=PARAMS,
        cost_estimate=cost(8 * count * width * hidden, 16 << 20),
    )(me, bias_o[None], gain[None], shift[None], bias_e[None], tok, own, got, *sources)
    return weights or out[5:7], (*out[:5], *out[5 + len(kept) :])


def ffn_backward_kernel(plan, rows, chips, me_ref, vec_ref, *refs):
    count = 2 if plan is None else len(plan)
    ins, pieces = refs[:5], refs[5 : 5 + count]
    result_out, grad_out, low_out, own_out, give_out, part_out, sum_out, wide_out = refs[
        5 + count : 13 + count
    ]
    (
        unit_ref, own, got, cot_ref, slope, expand, reduce,
        result_keep, grad_keep, low_keep, wide_keep,
        sem, expand_sem, reduce_sem, out_sem,
    ) = refs[13 + count :]
    me = me_ref[0]
    hidden = wide_keep.shape[1]
    loads = start_all(zip(ins, (unit_ref, own, got, cot_ref, slope)), sem)
    reduce_loads = start_weights(me, plan, rows, chips, pieces, 1, reduce, reduce_sem)
    expand_loads = start_weights(me, plan, rows, chips, pieces, 0, expand, expand_sem)
    gain_first, shift_first, bias_r, gain, shift = (vec_ref[i : i + 1, :] for i in range(5))
    wait_all(loads)
    mixed = (
        unit_ref[...] * gain_first
        + shift_first
        + (own[...].astype(F32) + got[...].astype(F32))
        + bias_r
    )
    out, unit, scale = ln_forward(mixed, gain, shift)
    cot = cot_ref[...].astype(F32)
    grad = ln_backward(cot, unit, scale, gain)
    result_keep[...] = out.astype(BF)
    grad_keep[...] = grad
    low_keep[...] = grad.astype(BF)
    copies = start_all(
        [(result_keep, result_out), (grad_keep, grad_out), (low_keep, low_out)], out_sem
    )
    for i, value in enumerate((cot * unit, cot, grad)):
        sum_out[i : i + 1, :] = jnp.sum(value, axis=0, keepdims=True)
    parts = len(reduce_loads)
    step = min(512, hidden // parts)
    for start in range(0, hidden, step):
        if start % (hidden // parts) == 0:
            wait_all(reduce_loads[start * parts // hidden])
        cols = slice(start, start + step)
        low = (dot(low_keep[...], reduce[:, cols]) * slope[:, cols].astype(F32)).astype(BF)
        wide_keep[:, cols] = low
        wide_out[:, cols] = jnp.sum(low.astype(F32), axis=0, keepdims=True)
    copies += start_all(halves(me, wide_keep, own_out, give_out), out_sem.at[pl.ds(3, 2)])
    for load in expand_loads:
        wait_all(load)
    part_out[...] = dot_nt(wide_keep[...], expand[...]).astype(BF)
    wait_all(copies)


def ffn_backward(me, ring, weights, chips, unit, own, got, cot, slope, vectors):
    count, width = unit.shape
    hidden = slope.shape[1]
    plan, sources = ffn_weights(ring, weights)
    scratch, sems = ffn_scratch(sources, width, hidden)
    block = pltpu.VMEM((count, width), BF)
    wide = pltpu.VMEM((count, hidden), BF)
    return pl.pallas_call(
        functools.partial(ffn_backward_kernel, plan, ring.rows, chips),
        out_shape=[
            jax.ShapeDtypeStruct((count, width), BF),
            jax.ShapeDtypeStruct((count, width), F32),
            jax.ShapeDtypeStruct((count, width), BF),
            jax.ShapeDtypeStruct((count, hidden // 2), BF),
            jax.ShapeDtypeStruct((count, hidden // 2), BF),
            jax.ShapeDtypeStruct((count, width), BF),
            jax.ShapeDtypeStruct((3, width), F32),
            jax.ShapeDtypeStruct((1, hidden), F32),
        ],
        in_specs=[SMEM, VMEM] + [ANY] * (5 + len(sources)),
        out_specs=[ANY] * 5 + [VMEM] * 3,
        scratch_shapes=[pltpu.VMEM((count, width), F32), block, block, block, wide]
        + scratch
        + [
            block,
            pltpu.VMEM((count, width), F32),
            block,
            wide,
            pltpu.SemaphoreType.DMA((5,)),
        ]
        + sems
        + [pltpu.SemaphoreType.DMA((5,))],
        compiler_params=PARAMS,
        cost_estimate=cost(8 * count * width * hidden, 16 << 20),
    )(me, vectors, unit, own, got, cot, slope, *sources)


def first_backward_kernel(
    mixed_ref, own_ref, got_ref, unit_ref, scale_ref, gain_ref, out_w_ref, *refs
):
    grad_out, low_out, ctx_out, sum_out = refs
    grad_normed = mixed_ref[...] + (own_ref[...].astype(F32) + got_ref[...].astype(F32))
    unit = unit_ref[...]
    grad = ln_backward(grad_normed, unit, scale_ref[...], gain_ref[...])
    low = grad.astype(BF)
    grad_out[...] = grad
    low_out[...] = low
    ctx_out[...] = dot(low, out_w_ref[...]).astype(BF)
    for i, value in enumerate((grad_normed * unit, grad_normed, grad)):
        sum_out[i : i + 1, :] = jnp.sum(value, axis=0, keepdims=True)


def first_backward(mixed, own, got, unit, scale, gain, full_attn):
    count, width = unit.shape
    local = full_attn.shape[1] // 4

    def whole(*shape):
        return pl.BlockSpec(shape, lambda i: (0, 0))

    return pl.pallas_call(
        first_backward_kernel,
        grid=(1,),
        out_shape=[
            jax.ShapeDtypeStruct((count, width), F32),
            jax.ShapeDtypeStruct((count, width), BF),
            jax.ShapeDtypeStruct((count, local), BF),
            jax.ShapeDtypeStruct((3, width), F32),
        ],
        in_specs=[whole(count, width)] * 4
        + [whole(count, 1), whole(1, width), pl.BlockSpec((width, local), lambda i: (0, 3))],
        out_specs=[whole(count, width)] * 2 + [whole(count, local), whole(3, width)],
        compiler_params=PARAMS,
        cost_estimate=cost(2 * count * width * local, 6 << 20),
    )(mixed, own, got, unit, scale, gain[None], full_attn)


def unpack_kernel(me_ref, total_ref, got_ref, q_out, k_out, v_out, o_out):
    rows, half = got_ref.shape
    own = total_ref[pl.ds(pl.multiple_of(rows * (me_ref[0] % 2), rows), rows), :]
    wide = half * 3 // 4
    first = me_ref[0] % 2 == 0
    outs = (q_out, k_out, v_out)
    for part in range(2):
        mine, got = own, got_ref[...].astype(F32)
        block = jnp.where(first, mine, got) if part == 0 else jnp.where(first, got, mine)
        for col in range(0, wide, 128):
            pair, which = divmod(part * wide + col, 384)
            outs[which // 128][:, 128 * pair : 128 * (pair + 1)] = block[:, col : col + 128]
        o_out[:, part * (half - wide) : (part + 1) * (half - wide)] = block[:, wide:]


def unpack(me, total, got):
    rows, half = got.shape
    return pl.pallas_call(
        unpack_kernel,
        out_shape=[jax.ShapeDtypeStruct((rows, half // 2), F32)] * 4,
        in_specs=[SMEM, VMEM, VMEM],
        out_specs=[VMEM] * 4,
        compiler_params=PARAMS,
        cost_estimate=cost(0, 12 * rows * half),
    )(me, total, got)


def pack_kernel(q_ref, k_ref, v_ref, o_ref, out_ref):
    local = q_ref.shape[1]
    for pair in range(local // 128):
        for i, ref in enumerate((q_ref, k_ref, v_ref)):
            col = 384 * pair + 128 * i
            out_ref[:, col : col + 128] = ref[:, 128 * pair : 128 * (pair + 1)]
    out_ref[:, 3 * local :] = o_ref[...]


def pack(w_query, w_key, w_value, w_output):
    rows, local = w_query.shape
    return pl.pallas_call(
        pack_kernel,
        out_shape=jax.ShapeDtypeStruct((rows, 4 * local), BF),
        in_specs=[VMEM] * 4,
        out_specs=VMEM,
        compiler_params=PARAMS,
    )(w_query, w_key, w_value, w_output)


def pair_major(parts):
    lead = parts[0].shape[:-1]
    stacked = jnp.stack([p.reshape(*lead, -1, 128) for p in parts], axis=-2)
    return stacked.reshape(*lead, -1)


def from_pair_major(array):
    lead = array.shape[:-1]
    stacked = array.reshape(*lead, -1, 3, 128)
    return [stacked[..., i, :].reshape(*lead, -1) for i in range(3)]


def tie(*arrays):
    return lax.optimization_barrier(arrays)


def ln_forward(values, gain, shift):
    centre = values - jnp.mean(values, axis=-1, keepdims=True)
    scale = lax.rsqrt(jnp.mean(centre * centre, axis=-1, keepdims=True) + NORM_EPS)
    unit = centre * scale
    return unit * gain + shift, unit, scale


def ln_backward(grad, unit, scale, gain):
    grad_unit = grad * gain
    along = jnp.mean(grad_unit * unit, axis=-1, keepdims=True)
    return scale * (grad_unit - jnp.mean(grad_unit, axis=-1, keepdims=True) - unit * along)


def ring_add_kernel(ahead_ref, behind_ref, up_ref, down_ref, up_out, down_out):
    rows = up_ref.shape[0]
    start = ahead_ref.shape[1] - rows
    for own, got, out, first in (
        (ahead_ref, up_ref, up_out, 0),
        (behind_ref, down_ref, down_out, start),
    ):
        total = own[0, first : first + rows].astype(F32) + got[...].astype(F32)
        out[first : first + rows, :] = total.astype(BF)
        if start:
            rest = slice(rows, None) if first == 0 else slice(0, start)
            out[rest, :] = own[0, rest]


def ring_add(blocks, step, up, down):
    chips, rows, cols = blocks.shape

    def whole(shape):
        return pl.BlockSpec(shape, lambda i: (0, 0))

    return pl.pallas_call(
        ring_add_kernel,
        grid=(1,),
        in_specs=[
            pl.BlockSpec((1, rows, cols), lambda i: (step, 0, 0)),
            pl.BlockSpec((1, rows, cols), lambda i: (chips - step, 0, 0)),
            whole(up.shape),
            whole(down.shape),
        ],
        out_specs=[whole((rows, cols))] * 2,
        out_shape=[jax.ShapeDtypeStruct((rows, cols), BF)] * 2,
        compiler_params=PARAMS,
        cost_estimate=cost(0, 10 * rows * cols),
    )(blocks, blocks, up, down)


class Links:
    def __init__(self):
        self.dp = lax.axis_size("dp")
        self.tensor = lax.axis_size("tensor")
        self.chips = self.dp // 2
        self.half_way = self.chips // 2
        self.order = list(range(0, self.chips, 2)) + list(range(1, self.chips, 2))[::-1]
        self.place = lax.axis_index("dp").astype(jnp.int32)
        self.core = self.place % 2
        self.me = self.place.reshape(1)

    def swap_core(self, array):
        return self.swap_dp(array, 1)

    def swap_dp(self, array, bit):
        return lax.ppermute(array, "dp", [(i, i ^ bit) for i in range(self.dp)])

    def swap_tensor(self, array, bit):
        return lax.ppermute(array, "tensor", [(i, i ^ bit) for i in range(self.tensor)])

    def along_ring(self, array, step):
        pairs = [
            (2 * self.order[i] + c, 2 * self.order[(i + step) % self.chips] + c)
            for i in range(self.chips)
            for c in range(2)
        ]
        return lax.ppermute(array, "dp", pairs)

    def bits(self, size):
        return [1 << b for b in range((size - 1).bit_length())]

    def gather_blocks(self, block):
        blocks = [block]
        for bit in self.bits(self.tensor):
            blocks = blocks + [self.swap_tensor(b, bit) for b in blocks]
        return blocks

    def sum_blocks(self, blocks, order, tied=True):
        if self.tensor == 2:
            blocks, got = list(blocks), [None, None]
            first, second = order
            got[second] = self.swap_tensor(blocks[first], 1)
            if tied:
                blocks[second], got[second] = tie(blocks[second], got[second])
            got[first] = self.swap_tensor(blocks[second], 1)
            return list(zip(blocks, got))
        for bit in self.bits(self.tensor):
            low = [b.astype(BF) for b in blocks]
            got = [self.swap_tensor(low[j ^ bit], bit) for j in range(len(low))]
            blocks = [a.astype(F32) + b.astype(F32) for a, b in zip(low, got)]
        return list(zip(low, got))

    def scatter_blocks(self, blocks):
        for bit in self.bits(self.tensor)[::-1]:
            got = [self.swap_tensor(blocks[j + bit].astype(BF), bit) for j in range(bit)]
            blocks = [blocks[j].astype(F32) + got[j].astype(F32) for j in range(bit)]
        return blocks[0]

    def sum_small(self, vector, axis):
        rows = vector.reshape(-1, 128)
        swap, size = (
            (self.swap_tensor, self.tensor) if axis == "tensor" else (self.swap_dp, self.dp)
        )
        for bit in self.bits(size):
            rows = rows + swap(rows, bit)
        return rows.reshape(vector.shape)

    def sum_near(self, rows):
        for bit in self.bits(self.dp)[:2]:
            rows = rows + self.swap_dp(rows, bit)
        return rows

    def sum_far(self, rows):
        far = [rows] + [self.swap_dp(rows, bit) for bit in range(4, self.dp, 4)]
        while len(far) > 1:
            far = [a + b for a, b in zip(far[::2], far[1::2])]
        return far[0]

    def own_half(self, array):
        half = array.shape[1] // 2
        return lax.dynamic_slice_in_dim(array, half * self.core, half, 1)

    def give_half(self, array):
        half = array.shape[1] // 2
        return self.swap_core(
            lax.dynamic_slice_in_dim(array, half * (1 - self.core), half, 1)
        )

    def swap_halves(self, total):
        rows = total.shape[0] // 2
        mine = lax.dynamic_slice_in_dim(total, rows * self.core, rows, 0)
        return mine, self.get_rows(total).astype(F32)

    def get_rows(self, total):
        rows = total.shape[0] // 2
        other = lax.dynamic_slice_in_dim(total, rows * (1 - self.core), rows, 0)
        return self.swap_core(other.astype(BF))

    def in_order(self, mine, got):
        first = self.core == 0
        return jnp.concatenate(
            [jnp.where(first, mine, got), jnp.where(first, got, mine)], axis=1
        )


class Gather:
    def __init__(self, links, shard):
        self.links = links
        self.rows = shard.shape[0]
        self.up = self.down = shard
        self.plan, self.pieces, self.step = [], [], 0
        self.arrive(shard, 0, 0)

    def arrive(self, block, distance, row):
        self.plan += [(distance, 0, row), (distance, 1, row)]
        self.pieces += [block, self.links.swap_core(block)]

    def hops(self):
        for _ in range(max(1, self.links.half_way // 4)):
            self.hop()

    def finish(self):
        while self.step < self.links.half_way:
            self.hop()

    def hop(self):
        if self.step == self.links.half_way:
            return
        self.step += 1
        half, last = self.rows // 2, self.step == self.links.half_way
        up, down = (self.up[:half], self.down[half:]) if last else (self.up, self.down)
        self.up = self.links.along_ring(up, 1)
        self.down = self.links.along_ring(down, -1)
        self.arrive(self.up, -self.step, 0)
        self.arrive(self.down, self.step, half if last else 0)

    def land(self, *arrays):
        out = tie(self.up, self.down, *arrays)
        self.up, self.down = out[:2]
        if self.step:
            self.pieces[-2], self.pieces[-4] = self.down, self.up
        return out[2:] if len(arrays) > 1 else out[2]

    def full(self):
        return assemble(self.links.me, self.plan, self.pieces, self.rows, self.links.chips)


class Scatter:
    def __init__(self, links, blocks):
        self.links, self.blocks, self.step = links, blocks, links.half_way
        self.arrived = None
        self.rows = blocks.shape[1]
        far = blocks[self.step]
        self.up, self.down = far[: self.rows // 2], far[self.rows // 2 :]

    def hops(self):
        for _ in range(max(1, self.links.half_way // 4)):
            self.hop()

    def finish(self):
        while self.step:
            self.hop()

    def hop(self):
        if not self.step:
            return
        links = self.links
        self.ready()
        up, down = links.along_ring(self.up, 1), links.along_ring(self.down, -1)
        self.step -= 1
        if self.step:
            self.arrived, self.up, self.down = (up, down), None, None
        else:
            self.up, self.down = up, down

    def ready(self):
        if self.up is None:
            self.up, self.down = ring_add(self.blocks, self.step, *self.arrived)

    def land(self, *arrays):
        moving = self.arrived if self.up is None else (self.up, self.down)
        out = tie(*moving, *arrays)
        if self.up is None:
            self.arrived = out[:2]
        else:
            self.up, self.down = out[:2]
        return out[2:] if len(arrays) > 1 else out[2]

    def total(self):
        self.finish()
        return self.blocks[0].astype(F32) + self.up.astype(F32) + self.down.astype(F32)


def add(a, b):
    return (a.astype(F32) + b.astype(F32)).astype(BF)


def gelu_pair(u):
    cdf = 0.5 * (1.0 + lax.erf(u * (0.5**0.5)))
    slope = cdf + u * jnp.exp(-0.5 * u * u) * 0.3989422804014327
    return u * cdf, slope


def shards(
    inputs,
    segments,
    w_query,
    w_key,
    w_value,
    w_output,
    w_expand,
    w_reduce,
    query_bias_vector,
    b_value,
    b_output,
    b_expand,
    b_reduce,
    gain_first,
    shift_first,
    gain_second,
    shift_second,
    cotangent,
):
    links = Links()
    parts = links.tensor
    rank = lax.axis_index("tensor")
    seqs, span, width = inputs.shape
    local = w_query.shape[1]
    hidden = w_expand.shape[1]
    length = span * parts
    chips = links.chips

    def flat(block):
        return block.reshape(seqs * span, block.shape[-1])

    def joined(blocks):
        return jnp.concatenate(
            [b.reshape(seqs, span, b.shape[-1]) for b in blocks], axis=1
        ).reshape(seqs * length, -1)

    def split(array):
        array = array.reshape(seqs, length, -1)
        return [flat(array[:, j * span : (j + 1) * span]) for j in range(parts)]

    attn = Gather(links, pack(w_query, w_key, w_value, w_output.T))
    attn.hops()
    token_blocks = [flat(b) for b in links.gather_blocks(inputs)]
    labels = jnp.concatenate(
        [
            lax.dynamic_slice_in_dim(segments, span * (rank ^ j), span, 1)
            for j in range(parts)
        ],
        axis=1,
    )
    rows = labels[:, None, :]
    qkv_bias = pair_major([query_bias_vector, jnp.zeros_like(b_value), b_value])[None]
    token_blocks[-1], rows, qkv_bias = attn.land(token_blocks[-1], rows, qkv_bias)
    attn.hops()
    ffn_shard, cotangent, token_blocks[-1] = attn.land(
        jnp.concatenate([w_expand, w_reduce.T], axis=1), cotangent, token_blocks[-1]
    )
    attn.hops()
    cotangent_blocks = [flat(b) for b in links.gather_blocks(cotangent)]
    ffn_shard = attn.land(ffn_shard)
    attn.finish()
    ffn = Gather(links, ffn_shard)
    ffn.hops()

    tokens = token_blocks if seqs == 1 else [joined(token_blocks)]
    tokens_pair = [links.swap_core(t) for t in tokens]

    full_attn, qkv = project(
        links.me, attn.plan, attn.pieces, attn.rows, chips, tokens, qkv_bias
    )
    ffn.hops()
    context, lse, partial = attend_forward(qkv, rows, full_attn, parts)
    partial = list(partial)
    cotangent_blocks[-1], partial[-1] = tie(cotangent_blocks[-1], partial[-1])
    partial[0] = ffn.land(partial[0])
    sums = links.sum_blocks(partial, range(parts)[::-1], tied=False)
    ffn.hops()
    sums[0] = (sums[0][0], ffn.land(sums[0][1]))
    ffn.finish()

    weights = None
    units, scales, normed_low, activated, slopes, partial = [], [], [], [], [], []
    for tok, (own, got) in zip(token_blocks, sums):
        weights, (unit, low, act, act_give, slope, scale, part) = ffn_forward(
            links.me, ffn, weights, chips, tok, own, got, b_output, gain_first, shift_first, b_expand
        )
        units.append(unit)
        scales.append(scale)
        normed_low.append(low)
        activated.append((act, act_give))
        slopes.append(slope)
        partial.append(part)

    sums = links.sum_blocks(partial, range(parts), tied=False)
    context_pair = links.give_half(context)
    got, context_pair = tie(sums[-1][1], context_pair)
    sums[-1] = (sums[-1][0], got)
    vectors = jnp.stack([gain_first, shift_first, b_reduce, gain_second, shift_second])
    grad_mixed, reduce_in, expand_low, partial = ([None] * parts for _ in range(4))
    grad_b_expand, small = 0.0, {}
    for j in range(parts)[::-1]:
        own, got = sums[j]
        out, grad, low, wide, wide_give, part, sums_mixed, sums_wide = ffn_backward(
            links.me, ffn, weights, chips, units[j], own, got, cotangent_blocks[j], slopes[j], vectors
        )
        if j == 0:
            result = out.reshape(seqs, span, width)
            small["second"] = sums_mixed
        grad_b_expand = grad_b_expand + sums_wide[0]
        grad_mixed[j], reduce_in[j], expand_low[j], partial[j] = (
            grad, low, (wide, wide_give), part,
        )

    def cut_cores(wide, narrow):
        return [(w, n, False, 0) for w, (n, _) in zip(wide, narrow)] + [
            (links.swap_core(w), links.swap_core(n), False, 0)
            for w, (_, n) in zip(wide, narrow)
        ]

    def both_cores(wide, narrow):
        return [(w, n, True, 0) for w, n in zip(wide, narrow)] + [
            (links.swap_core(w), links.give_half(n), False, 0) for w, n in zip(wide, narrow)
        ]

    def rows_of(wide, narrow, pair):
        return [(w, narrow, True, j) for j, w in enumerate(wide)] + [
            (w, pair, False, j) for j, w in enumerate([links.swap_core(w) for w in wide])
        ]

    sums = links.sum_blocks(partial, range(parts)[::-1])
    grad_attended, attn_low, grad_context = [], [], []

    def first(j):
        grad, low, grad_ctx, sums_first = first_backward(
            grad_mixed[j], *sums[j], units[j], scales[j], gain_first, full_attn
        )
        if j == 0:
            small["first"] = sums_first
        grad_attended.append(grad)
        attn_low.append(low)
        grad_context.append(grad_ctx)

    first(0)
    early = links.sum_small(jnp.concatenate([small["second"], small["first"]]), "tensor")
    terms = [cut_cores(reduce_in, activated), cut_cores(normed_low, expand_low)]
    wide, grad_context[0] = tie(terms[0][0][0], grad_context[0])
    terms[0][0] = (wide, *terms[0][0][1:])
    blocks = pair_grads(links.me, chips, terms)
    last = sums[parts - 1]
    blocks, early, got = tie(blocks, early, last[1])
    sums[parts - 1] = (last[0], got)
    ffn_sum = Scatter(links, blocks)
    ffn_sum.hops()
    for j in range(1, parts):
        first(j)
    grad_context[-1] = ffn_sum.land(grad_context[-1])
    ffn_sum.hops()
    grad_qkv, bias_sums, give, back_low = attend_backward(
        links.me, qkv, rows, lse, full_attn, grad_context
    )
    grad_qkv, bias_sums = ffn_sum.land(grad_qkv, bias_sums)
    vector = jnp.concatenate([early.reshape(-1), grad_b_expand, bias_sums]).reshape(-1, 128)
    vector = links.sum_near(vector)
    ffn_sum.hops()
    pair = links.give_half(grad_qkv) if give is None else links.swap_core(give)
    if seqs == 1:
        context_terms = rows_of(attn_low, context, context_pair)
        qkv_terms = [(t, grad_qkv, True, j) for j, t in enumerate(tokens)] + [
            (t, pair, False, j) for j, t in enumerate(tokens_pair)
        ]
    else:
        context_terms = both_cores(attn_low, split(context))
        qkv_terms = [
            (tokens[0], grad_qkv, True, 0),
            (tokens_pair[0], pair, False, 0),
        ]
    blocks = pair_grads(links.me, chips, [qkv_terms, context_terms])
    blocks, vector = ffn_sum.land(blocks, vector)
    attn_sum = Scatter(links, blocks)
    attn_sum.hops()
    ffn_sum.finish()
    vector = links.sum_far(vector)
    back_low[-1] = attn_sum.land(back_low[-1])
    attn_sum.hops()
    grad_inputs = grad_attended[0] + links.scatter_blocks(back_low)
    vector = attn_sum.land(vector)
    attn_sum.hops()
    grad_inputs = attn_sum.land(grad_inputs)
    attn_sum.finish()
    vector = vector.reshape(-1)
    mine, got = links.swap_halves(ffn_sum.total())
    half_hidden, half_local = hidden // 2, local // 2
    grad_reduce = links.in_order(mine[:, :half_hidden], got[:, :half_hidden])
    grad_expand = links.in_order(mine[:, half_hidden:], got[:, half_hidden:])
    total = attn_sum.total()
    if local % 256 == 0:
        grad_wq, grad_wk, grad_wv, grad_output = unpack(
            links.me, total, links.get_rows(total)
        )
    else:
        mine, got = links.swap_halves(total)
        grad_wq, grad_wk, grad_wv = from_pair_major(
            links.in_order(mine[:, : 3 * half_local], got[:, : 3 * half_local])
        )
        grad_output = links.in_order(mine[:, 3 * half_local :], got[:, 3 * half_local :])

    early = vector[: 6 * width].reshape(6, width)
    middle = vector[6 * width : 6 * width + hidden]
    grad_bq, _, grad_bv = from_pair_major(vector[6 * width + hidden :])
    return (
        result,
        grad_inputs.reshape(seqs, span, width),
        grad_wq,
        grad_wk,
        grad_wv,
        grad_output.T,
        grad_expand,
        grad_reduce.T,
        grad_bq,
        grad_bv,
        early[5],
        middle,
        early[2],
        early[3],
        early[4],
        early[0],
        early[1],
    )


def solution(mesh):
    return jax.shard_map(
        shards,
        mesh=mesh,
        in_specs=(
            P("dp", "tensor", None),
            P("dp", None),
            P("dp", "tensor"),
            P("dp", "tensor"),
            P("dp", "tensor"),
            P("tensor", "dp"),
            P("dp", "tensor"),
            P("tensor", "dp"),
            P("tensor"),
            P("tensor"),
            P(),
            P("tensor"),
            P(),
            P(),
            P(),
            P(),
            P(),
            P("dp", "tensor", None),
        ),
        out_specs=(
            P("dp", "tensor", None),
            P("dp", "tensor", None),
            P("dp", "tensor"),
            P("dp", "tensor"),
            P("dp", "tensor"),
            P("tensor", "dp"),
            P("dp", "tensor"),
            P("tensor", "dp"),
            P("tensor"),
            P("tensor"),
            P(),
            P("tensor"),
            P(),
            P(),
            P(),
            P(),
            P(),
        ),
        check_vma=False,
    )
```

profile of v0, /device:TPU:0, one launch (start us, length us, event | category | flops | bytes accessed | tf_op | source)
XLA Modules:
  0.0 271.4 jit_solution(14740558754649600712)
XLA Ops:
  0.7 3.0 %collective-permute-start.2 = (bf16[1,256,1024]{2,1,0:T(8,128)(2,1)}, bf16[1,256,1024]{2,1,0:T(8,128)(2,1)S(1)}, u32[]{:S(2)}, u32[]{:S(2)}) collective-permute-start(bf16[1,256,1024]{2,1,0:T(8,128)(2,1)} %param.18), channel_id=1, source_target_pairs={{0,1},{1,0},{2,3},{3,2},{4,5},{5,4},{6,7},{7,6},{8,9},{9,8},{10,11... | collective-permute-start | bytes 1572872 | tf_op jit(solution)/shard_map/ppermute | solution.py:777
  10.1 3.2 %collective-permute-done.refs_4_ = bf16[64,2048]{1,0:T(8,128)(2,1)S(1)} collective-permute-done((bf16[64,2048]{1,0:T(8,128)(2,1)}, bf16[64,2048]{1,0:T(8,128)(2,1)S(1)}, u32[]{:S(2)}, u32[]{:S(2)}) %collective-permute-start) | collective-permute-done | bytes 262176 | tf_op jit(solution)/shard_map/ppermute | solution.py:785
  18.9 4.4 %collective-permute-done.3.refs_8_ = bf16[64,2048]{1,0:T(8,128)(2,1)S(1)} collective-permute-done((bf16[64,2048]{1,0:T(8,128)(2,1)S(1)}, bf16[64,2048]{1,0:T(8,128)(2,1)S(1)}, u32[]{:S(2)}, u32[]{:S(2)}) %collective-permute-start.3) | collective-permute-done | bytes 262176 | tf_op jit(solution)/shard_map/ppermute | solution.py:785
  27.1 3.8 %collective-permute-done.5.refs_12_ = bf16[64,2048]{1,0:T(8,128)(2,1)S(1)} collective-permute-done((bf16[64,2048]{1,0:T(8,128)(2,1)S(1)}, bf16[64,2048]{1,0:T(8,128)(2,1)S(1)}, u32[]{:S(2)}, u32[]{:S(2)}) %collective-permute-start.5) | collective-permute-done | bytes 262176 | tf_op jit(solution)/shard_map/ppermute | solution.py:785
  40.8 5.4 %collective-permute-done.9.refs_7_ = bf16[64,4096]{1,0:T(8,128)(2,1)S(1)} collective-permute-done((bf16[64,4096]{1,0:T(8,128)(2,1)S(1)}, bf16[64,4096]{1,0:T(8,128)(2,1)S(1)}, u32[]{:S(2)}, u32[]{:S(2)}) %collective-permute-start.9) | collective-permute-done | bytes 524320 | tf_op jit(solution)/shard_map/ppermute | solution.py:785
  53.3 7.0 %shard_map.306 = (bf16[1024,2048]{1,0:T(8,128)(2,1)}, bf16[512,1536]{1,0:T(8,128)(2,1)}) custom-call(s32[1]{0:T(128)} %bitcast.me_ref, f32[1,1536]{1,0:T(1,128)} %broadcast_in_dim_reshape.3.bias_ref, bf16[256,1024]{1,0:T(8,128)(2,1)} %bitcast.61, bf16[256,1024]{1,0:T(8,128)(2,1)} %bitcast.66, bf16[64,2048]{1,0:T(8,128)(2,1)} %shard_map.305.refs_2_, ...), custom_call_target="tpu_custom_call" | custom-call | flops 1572864 | bytes 16384 | tf_op jit(solution)/shard_map/pallas_call | solution.py:284
  60.4 8.8 %shard_map.307 = (bf16[512,512]{1,0:T(8,128)(2,1)}, f32[4,2,512]{2,1,0:T(2,128)}, bf16[256,1024]{1,0:T(8,128)(2,1)}, bf16[256,1024]{1,0:T(8,128)(2,1)}) custom-call(bf16[512,1536]{1,0:T(8,128)(2,1)} %get-tuple-element.141.qkv_ref, s32[1,1,512]{2,1,0:T(1,128)} %add_bitcast_fusion.row_ref, bf16[1024,2048]{1,0:T(8,128)(2,1)} %get-tuple-element.143.out_w_ref.w_ref), custom_call_target="tpu_custom_call" | custom-call | flops 3145728 | bytes 8192 | tf_op jit(solution)/shard_map/pallas_call | solution.py:79
  73.4 10.0 %collective-permute-done.25.refs_2_ = bf16[256,1024]{1,0:T(8,128)(2,1)S(1)} collective-permute-done((bf16[256,1024]{1,0:T(8,128)(2,1)}, bf16[256,1024]{1,0:T(8,128)(2,1)S(1)}, u32[]{:S(2)}, u32[]{:S(2)}) %collective-permute-start.25) | collective-permute-done | bytes 524320 | tf_op jit(solution)/shard_map/ppermute | solution.py:777
  89.3 5.6 %collective-permute-done.33.refs_17_ = bf16[32,4096]{1,0:T(8,128)(2,1)S(1)} collective-permute-done((bf16[32,4096]{1,0:T(8,128)(2,1)S(1)}, bf16[32,4096]{1,0:T(8,128)(2,1)S(1)}, u32[]{:S(2)}, u32[]{:S(2)}) %collective-permute-start.33) | collective-permute-done | bytes 262176 | tf_op jit(solution)/shard_map/ppermute | solution.py:785
  99.1 12.2 %shard_map.308 = (f32[256,1024]{1,0:T(8,128)}, bf16[256,1024]{1,0:T(8,128)(2,1)}, bf16[256,1024]{1,0:T(8,128)(2,1)}, bf16[256,1024]{1,0:T(8,128)(2,1)}, bf16[256...) custom-call(s32[1]{0:T(128)} %bitcast.me_ref, ...), custom_call_target="tpu_custom_call" | custom-call | flops 4194304 | bytes 16384 | tf_op jit(solution)/shard_map/pallas_call | solution.py:487
  112.7 8.5 %shard_map.309 = (f32[256,1024]{1,0:T(8,128)}, bf16[256,1024]{1,0:T(8,128)(2,1)}, bf16[256,1024]{1,0:T(8,128)(2,1)}, bf16[256,1024]{1,0:T(8,128)(2,1)}, bf16[256...) custom-call(s32[1]{0:T(128)} %bitcast.me_ref, f32[1,1024]{1,0:T(1,128)} %bitcast.90, ...), custom_call_target="tpu_custom_call" | custom-call | flops 4194304 | bytes 16384 | tf_op jit(solution)/shard_map/pallas_call | solution.py:487
  126.5 8.9 %shard_map.311 = (bf16[256,1024]{1,0:T(8,128)(2,1)}, f32[256,1024]{1,0:T(8,128)}, bf16[256,1024]{1,0:T(8,128)(2,1)}, bf16[256,1024]{1,0:T(8,128)(2,1)}, bf16[256...) custom-call(s32[1]{0:T(128)} %bitcast.me_ref, ...), custom_call_target="tpu_custom_call" | custom-call | flops 4194304 | bytes 16384 | tf_op jit(solution)/shard_map/pallas_call | solution.py:578
  138.1 9.0 %shard_map.310 = (bf16[256,1024]{1,0:T(8,128)(2,1)}, f32[256,1024]{1,0:T(8,128)}, bf16[256,1024]{1,0:T(8,128)(2,1)}, bf16[256,1024]{1,0:T(8,128)(2,1)}, bf16[256...) custom-call(s32[1]{0:T(128)} %bitcast.me_ref, ...), custom_call_target="tpu_custom_call" | custom-call | flops 4194304 | bytes 16384 | tf_op jit(solution)/shard_map/pallas_call | solution.py:578
  149.0 4.3 %shard_map.312 = (f32[256,1024]{1,0:T(8,128)}, bf16[256,1024]{1,0:T(8,128)(2,1)}, bf16[256,512]{1,0:T(8,128)(2,1)}, f32[3,1024]{1,0:T(4,128)}) custom-call(f32[256,1024]{1,0:T(8,128)} %get-tuple-element.162.mixed_ref, bf16[256,1024]{1,0:T(8,128)(2,1)} %get-tuple-element.170.own_ref, bf16[256,1024]{1,0:T(8,128)(2,1)} %collective-permute-done.41.got_ref, ...), custom_call_target="tpu_custom_call" | custom-call | flops 262144 | bytes 6144 | tf_op jit(solution)/shard_map/pallas_call | solution.py:630
  156.4 10.9 %shard_map.313.ahead_ref.behind_ref = bf16[8,128,2048]{2,1,0:T(8,128)(2,1)} custom-call(s32[1]{0:T(128)} %bitcast.me_ref, bf16[256,1024]{1,0:T(8,128)(2,1)} %get-tuple-element.174.refs_0_.refs_1_, bf16[256,1024]{1,0:T(8,128)(2,1)} %get-tuple-element.174.refs_0_.refs_1_, bf16[256,1024]{1,0:T(8,128)(2,1)} %get-tuple-element.175.refs_2_, ...), custom_call_target="tpu_custom_call" | custom-call | flops 4194304 | bytes 8192 | tf_op jit(solution)/shard_map/pallas_call | solution.py:355
  170.8 4.3 %shard_map.314 = (f32[256,1024]{1,0:T(8,128)}, bf16[256,1024]{1,0:T(8,128)(2,1)}, bf16[256,512]{1,0:T(8,128)(2,1)}, f32[3,1024]{1,0:T(4,128)}) custom-call(f32[256,1024]{1,0:T(8,128)} %get-tuple-element.189.mixed_ref, bf16[256,1024]{1,0:T(8,128)(2,1)} %get-tuple-element.169.own_ref, bf16[256,1024]{1,0:T(8,128)(2,1)} %copy-done.38, ...), custom_call_target="tpu_custom_call" | custom-call | flops 262144 | bytes 6144 | tf_op jit(solution)/shard_map/pallas_call | solution.py:630
  179.0 2.5 shard_map.315
  184.1 13.9 %shard_map.316 = (bf16[512,1536]{1,0:T(8,128)(2,1)}, f32[1,1,1536]{2,1,0:T(1,128)}, f32[256,1024]{1,0:T(8,128)}, bf16[256,1024]{1,0:T(8,128)(2,1)}, bf16[512,768]{1,0:T(8,128)(2,1)}) custom-call(s32[1]{0:T(128)} %bitcast.me_ref, bf16[512,1536]{1,0:T(8,128)(2,1)} %get-tuple-element.141.qkv_ref, s32[1,1,512]{2,1,0:T(1,128)} %add_bitcast_fusion.row_ref, ...), custom_call_target="tpu_custom_call" | custom-call | flops 5242880 | bytes 8192 | tf_op jit(solution)/shard_map/pallas_call | solution.py:175
  201.0 2.6 shard_map.317
  207.7 8.2 %shard_map.318.ahead_ref.behind_ref = bf16[8,128,1024]{2,1,0:T(8,128)(2,1)} custom-call(s32[1]{0:T(128)} %bitcast.me_ref, bf16[256,1024]{1,0:T(8,128)(2,1)} %bitcast.63, bf16[256,1024]{1,0:T(8,128)(2,1)} %bitcast.64, bf16[512,1536]{1,0:T(8,128)(2,1)} %get-tuple-element.206.refs_2_.refs_5_, bf16[256,1024]{1,0:T(8,128)(2,1)} %bitcast.68, ...), custom_call_target="tpu_custom_call" | custom-call | flops 2097152 | bytes 8192 | tf_op jit(solution)/shard_map/pallas_call | solution.py:355
  223.4 2.5 collective-permute-start.71
  230.5 2.6 shard_map.323
  244.9 3.5 %collective-permute-done.78 = bf16[128,2048]{1,0:T(8,128)(2,1)} collective-permute-done((bf16[128,2048]{1,0:T(8,128)(2,1)}, bf16[128,2048]{1,0:T(8,128)(2,1)}, u32[]{:S(2)}, u32[]{:S(2)}) %collective-permute-start.78) | collective-permute-done | bytes 524320 | tf_op jit(solution)/shard_map/ppermute | solution.py:785
  259.7 6.1 %collective-permute-done.75 = bf16[128,1024]{1,0:T(8,128)(2,1)S(1)} collective-permute-done((bf16[128,1024]{1,0:T(8,128)(2,1)}, bf16[128,1024]{1,0:T(8,128)(2,1)S(1)}, u32[]{:S(2)}, u32[]{:S(2)}) %collective-permute-start.75) | collective-permute-done | bytes 262176 | tf_op jit(solution)/shard_map/ppermute | solution.py:785
  (347 shorter events, 118.6 us)
Async XLA Ops:
  0.7 15.1 %collective-permute-start.2 = (bf16[1,256,1024]{2,1,0:T(8,128)(2,1)}, bf16[1,256,1024]{2,1,0:T(8,128)(2,1)S(1)}, u32[]{:S(2)}, u32[]{:S(2)}) collective-permute-start(bf16[1,256,1024]{2,1,0:T(8,128)(2,1)} %param.18), channel_id=1, source_target_pairs={{0,1},{1,0},{2,3},{3,2},{4,5},{5,4},{6,7},{7,6},{8,9},{9,8},{10,11... | collective-permute-start | bytes 1572872 | tf_op jit(solution)/shard_map/ppermute | solution.py:777
  39.3 29.8 %collective-permute-start.24 = (bf16[1,256,1024]{2,1,0:T(8,128)(2,1)}, bf16[1,256,1024]{2,1,0:T(8,128)(2,1)S(1)}, u32[]{:S(2)}, u32[]{:S(2)}) collective-permute-start(bf16[1,256,1024]{2,1,0:T(8,128)(2,1)} %param.35), channel_id=1, source_target_pairs={{0,1},{1,0},{2,3},{3,2},{4,5},{5,4},{6,7},{7,6},{8,9},{9,8},{10,11... | collective-permute-start | bytes 1572872 | tf_op jit(solution)/shard_map/ppermute | solution.py:777
  46.2 24.6 %collective-permute-start.10 = (bf16[64,4096]{1,0:T(8,128)(2,1)S(1)}, bf16[64,4096]{1,0:T(8,128)(2,1)}, u32[]{:S(2)}, u32[]{:S(2)}) collective-permute-start(bf16[64,4096]{1,0:T(8,128)(2,1)S(1)} %collective-permute-done.9.refs_7_), channel_id=1, source_target_pairs={{0,4},{2,6},{8,0},{10,2},{16,8},{18,10},{24,16},{26,18},{28,24},{3... | collective-permute-start | bytes 1572872 | tf_op jit(solution)/shard_map/ppermute | solution.py:785
  46.7 24.2 %collective-permute-start.8 = (bf16[64,4096]{1,0:T(8,128)(2,1)S(1)}, bf16[64,4096]{1,0:T(8,128)(2,1)}, u32[]{:S(2)}, u32[]{:S(2)}) collective-permute-start(bf16[64,4096]{1,0:T(8,128)(2,1)S(1)} %collective-permute-done.7.refs_5_), channel_id=1, source_target_pairs={{0,8},{2,10},{8,16},{10,18},{16,24},{18,26},{24,28},{26,30},{28,20... | collective-permute-start | bytes 1572872 | tf_op jit(solution)/shard_map/ppermute | solution.py:785
  69.1 14.3 %collective-permute-start.25 = (bf16[256,1024]{1,0:T(8,128)(2,1)}, bf16[256,1024]{1,0:T(8,128)(2,1)S(1)}, u32[]{:S(2)}, u32[]{:S(2)}) collective-permute-start(bf16[256,1024]{1,0:T(8,128)(2,1)} %get-tuple-element.150.refs_1_), channel_id=1, source_target_pairs={{0,1},{1,0},{2,3},{3,2},{4,5},{5,4},{6,7},{7,6},{8,9},{9,8},{10,11... | collective-permute-start | bytes 1572872 | tf_op jit(solution)/shard_map/ppermute | solution.py:777
  70.9 13.9 %collective-permute-start.22 = (bf16[64,4096]{1,0:T(8,128)(2,1)}, bf16[64,4096]{1,0:T(8,128)(2,1)S(1)}, u32[]{:S(2)}, u32[]{:S(2)}) collective-permute-start(bf16[64,4096]{1,0:T(8,128)(2,1)} %collective-permute-done.8.refs_9_), channel_id=1, source_target_pairs={{0,8},{2,10},{8,16},{10,18},{16,24},{18,26},{24,28},{26,30},{28,20... | collective-permute-start | bytes 1572872 | tf_op jit(solution)/shard_map/ppermute | solution.py:785
  72.9 15.1 %collective-permute-start.27 = (bf16[64,4096]{1,0:T(8,128)(2,1)S(1)}, bf16[64,4096]{1,0:T(8,128)(2,1)S(1)}, u32[]{:S(2)}, u32[]{:S(2)}) collective-permute-start(bf16[64,4096]{1,0:T(8,128)(2,1)S(1)} %collective-permute-done.7.refs_5_), channel_id=1, source_target_pairs={{0,2},{2,0},{4,6},{6,4},{8,10},{10,8},{12,14},{14,12},{16,18},{18,... | collective-permute-start | bytes 1572872 | tf_op jit(solution)/shard_map/ppermute | solution.py:774
  88.8 23.1 %collective-permute-start.37 = (bf16[256,1024]{1,0:T(8,128)(2,1)}, bf16[256,1024]{1,0:T(8,128)(2,1)S(1)}, u32[]{:S(2)}, u32[]{:S(2)}) collective-permute-start(bf16[256,1024]{1,0:T(8,128)(2,1)} %get-tuple-element.145.refs_1_), channel_id=1, source_target_pairs={{0,1},{1,0},{2,3},{3,2},{4,5},{5,4},{6,7},{7,6},{8,9},{9,8},{10,11... | collective-permute-start | bytes 1572872 | tf_op jit(solution)/shard_map/ppermute | solution.py:777
  111.3 15.1 %collective-permute-start.39 = (bf16[256,1024]{1,0:T(8,128)(2,1)}, bf16[256,1024]{1,0:T(8,128)(2,1)}, u32[]{:S(2)}, u32[]{:S(2)}) collective-permute-start(bf16[256,1024]{1,0:T(8,128)(2,1)} %get-tuple-element.155.refs_1_), channel_id=1, source_target_pairs={{0,1},{1,0},{2,3},{3,2},{4,5},{5,4},{6,7},{7,6},{8,9},{9,8},{10,11... | collective-permute-start | bytes 1572872 | tf_op jit(solution)/shard_map/ppermute | solution.py:777
  121.2 15.6 %collective-permute-start.38 = (bf16[256,1024]{1,0:T(8,128)(2,1)}, bf16[256,1024]{1,0:T(8,128)(2,1)S(1)}, u32[]{:S(2)}, u32[]{:S(2)}) collective-permute-start(bf16[256,1024]{1,0:T(8,128)(2,1)} %get-tuple-element.158.refs_1_), channel_id=1, source_target_pairs={{0,1},{1,0},{2,3},{3,2},{4,5},{5,4},{6,7},{7,6},{8,9},{9,8},{10,11... | collective-permute-start | bytes 1572872 | tf_op jit(solution)/shard_map/ppermute | solution.py:777
  122.9 14.8 %collective-permute-start.45 = (bf16[256,1024]{1,0:T(8,128)(2,1)}, bf16[256,1024]{1,0:T(8,128)(2,1)S(1)}, u32[]{:S(2)}, u32[]{:S(2)}) collective-permute-start(bf16[256,1024]{1,0:T(8,128)(2,1)} %get-tuple-element.179), channel_id=1, source_target_pairs={{0,2},{2,0},{4,6},{6,4},{8,10},{10,8},{12,14},{14,12},{16,18},{18,... | collective-permute-start | bytes 1572872 | tf_op jit(solution)/shard_map/ppermute | solution.py:774
  124.1 23.2 %collective-permute-start.48 = (bf16[256,1024]{1,0:T(8,128)(2,1)}, bf16[256,1024]{1,0:T(8,128)(2,1)S(1)}, u32[]{:S(2)}, u32[]{:S(2)}) collective-permute-start(bf16[256,1024]{1,0:T(8,128)(2,1)} %get-tuple-element.182.refs_15_.refs_16_), channel_id=1, source_target_pairs={{0,2},{2,0},{4,6},{6,4},{8,10},{10,8},{12,14},{14,12},{16,18},{18,... | collective-permute-start | bytes 1572872 | tf_op jit(solution)/shard_map/ppermute | solution.py:774
  124.4 23.0 %collective-permute-start.43 = (bf16[256,1024]{1,0:T(8,128)(2,1)}, bf16[256,1024]{1,0:T(8,128)(2,1)S(1)}, u32[]{:S(2)}, u32[]{:S(2)}) collective-permute-start(bf16[256,1024]{1,0:T(8,128)(2,1)} %get-tuple-element.178), channel_id=1, source_target_pairs={{0,2},{2,0},{4,6},{6,4},{8,10},{10,8},{12,14},{14,12},{16,18},{18,... | collective-permute-start | bytes 1572872 | tf_op jit(solution)/shard_map/ppermute | solution.py:774
  137.6 16.4 %collective-permute-start.44 = (bf16[256,1024]{1,0:T(8,128)(2,1)}, bf16[256,1024]{1,0:T(8,128)(2,1)S(1)}, u32[]{:S(2)}, u32[]{:S(2)}) collective-permute-start(bf16[256,1024]{1,0:T(8,128)(2,1)} %get-tuple-element.176.refs_3_.refs_4_), channel_id=1, source_target_pairs={{0,2},{2,0},{4,6},{6,4},{8,10},{10,8},{12,14},{14,12},{16,18},{18,... | collective-permute-start | bytes 1572872 | tf_op jit(solution)/shard_map/ppermute | solution.py:774
  148.4 19.0 %collective-permute-start.51 = (bf16[256,1024]{1,0:T(8,128)(2,1)}, bf16[256,1024]{1,0:T(8,128)(2,1)S(1)}, u32[]{:S(2)}, u32[]{:S(2)}) collective-permute-start(bf16[256,1024]{1,0:T(8,128)(2,1)} %get-tuple-element.170.own_ref), channel_id=1, source_target_pairs={{0,1},{1,0},{2,3},{3,2},{4,5},{5,4},{6,7},{7,6},{8,9},{9,8},{10,11... | collective-permute-start | bytes 1572872 | tf_op jit(solution)/shard_map/ppermute | solution.py:777
  181.5 17.2 %collective-permute-start.54 = (bf16[128,2048]{1,0:T(8,128)(2,1)}, bf16[128,2048]{1,0:T(8,128)(2,1)S(1)}, u32[]{:S(2)}, u32[]{:S(2)}) collective-permute-start(bf16[128,2048]{1,0:T(8,128)(2,1)} %get-tuple-element.195), channel_id=1, source_target_pairs={{0,8},{2,10},{8,16},{10,18},{16,24},{18,26},{24,28},{26,30},{28,20... | collective-permute-start | bytes 1572872 | tf_op jit(solution)/shard_map/ppermute | solution.py:785
  182.1 16.6 %collective-permute-start.55 = (bf16[128,2048]{1,0:T(8,128)(2,1)}, bf16[128,2048]{1,0:T(8,128)(2,1)}, u32[]{:S(2)}, u32[]{:S(2)}) collective-permute-start(bf16[128,2048]{1,0:T(8,128)(2,1)} %get-tuple-element.196), channel_id=1, source_target_pairs={{0,4},{2,6},{8,0},{10,2},{16,8},{18,10},{24,16},{26,18},{28,24},{3... | collective-permute-start | bytes 1572872 | tf_op jit(solution)/shard_map/ppermute | solution.py:785
  183.5 16.9 %collective-permute-start.58 = (bf16[256,1024]{1,0:T(8,128)(2,1)S(1)}, bf16[256,1024]{1,0:T(8,128)(2,1)S(1)}, u32[]{:S(2)}, u32[]{:S(2)}) collective-permute-start(bf16[256,1024]{1,0:T(8,128)(2,1)S(1)} %bitcast.65), channel_id=1, source_target_pairs={{0,2},{2,0},{4,6},{6,4},{8,10},{10,8},{12,14},{14,12},{16,18},{18,... | collective-permute-start | bytes 1572872 | tf_op jit(solution)/shard_map/ppermute | solution.py:774
  183.5 20.1 %collective-permute-start.60 = (bf16[256,1024]{1,0:T(8,128)(2,1)S(1)}, bf16[256,1024]{1,0:T(8,128)(2,1)}, u32[]{:S(2)}, u32[]{:S(2)}) collective-permute-start(bf16[256,1024]{1,0:T(8,128)(2,1)S(1)} %bitcast.70), channel_id=1, source_target_pairs={{0,2},{2,0},{4,6},{6,4},{8,10},{10,8},{12,14},{14,12},{16,18},{18,... | collective-permute-start | bytes 1572872 | tf_op jit(solution)/shard_map/ppermute | solution.py:774
  203.6 14.2 %collective-permute-start.56 = (bf16[128,2048]{1,0:T(8,128)(2,1)}, bf16[128,2048]{1,0:T(8,128)(2,1)S(1)}, u32[]{:S(2)}, u32[]{:S(2)}) collective-permute-start(bf16[128,2048]{1,0:T(8,128)(2,1)} %get-tuple-element.204), channel_id=1, source_target_pairs={{0,8},{2,10},{8,16},{10,18},{16,24},{18,26},{24,28},{26,30},{28,20... | collective-permute-start | bytes 1572872 | tf_op jit(solution)/shard_map/ppermute | solution.py:785
  204.1 14.1 %collective-permute-start.57 = (bf16[128,2048]{1,0:T(8,128)(2,1)}, bf16[128,2048]{1,0:T(8,128)(2,1)S(1)}, u32[]{:S(2)}, u32[]{:S(2)}) collective-permute-start(bf16[128,2048]{1,0:T(8,128)(2,1)} %get-tuple-element.205), channel_id=1, source_target_pairs={{0,4},{2,6},{8,0},{10,2},{16,8},{18,10},{24,16},{26,18},{28,24},{3... | collective-permute-start | bytes 1572872 | tf_op jit(solution)/shard_map/ppermute | solution.py:785
  233.2 15.2 %collective-permute-start.78 = (bf16[128,2048]{1,0:T(8,128)(2,1)}, bf16[128,2048]{1,0:T(8,128)(2,1)}, u32[]{:S(2)}, u32[]{:S(2)}) collective-permute-start(bf16[128,2048]{1,0:T(8,128)(2,1)} %get-tuple-element.240), channel_id=1, source_target_pairs={{0,8},{2,10},{8,16},{10,18},{16,24},{18,26},{24,28},{26,30},{28,20... | collective-permute-start | bytes 1572872 | tf_op jit(solution)/shard_map/ppermute | solution.py:785
  234.3 15.9 %collective-permute-start.79 = (bf16[128,2048]{1,0:T(8,128)(2,1)}, bf16[128,2048]{1,0:T(8,128)(2,1)}, u32[]{:S(2)}, u32[]{:S(2)}) collective-permute-start(bf16[128,2048]{1,0:T(8,128)(2,1)} %get-tuple-element.241), channel_id=1, source_target_pairs={{0,4},{2,6},{8,0},{10,2},{16,8},{18,10},{24,16},{26,18},{28,24},{3... | collective-permute-start | bytes 1572872 | tf_op jit(solution)/shard_map/ppermute | solution.py:785
  235.3 16.6 %collective-permute-start.74 = (bf16[256,1024]{1,0:T(8,128)(2,1)}, bf16[256,1024]{1,0:T(8,128)(2,1)}, u32[]{:S(2)}, u32[]{:S(2)}) collective-permute-start(bf16[256,1024]{1,0:T(8,128)(2,1)} %get-tuple-element.228), channel_id=1, source_target_pairs={{0,1},{1,0},{2,3},{3,2},{4,5},{5,4},{6,7},{7,6},{8,9},{9,8},{10,11... | collective-permute-start | bytes 1572872 | tf_op jit(solution)/shard_map/ppermute | solution.py:777
  (133 other events, 1186.5 us)
where the time goes:
time: 272 us; the launch traced here: 271 us
  Pallas kernels  113 us (42%)
  waiting for transfers between devices  72.3 us (27%)
  starting transfers between devices  56.2 us (21%)
  local copies, waits for them, and re-layouts  18 us (7%)
  other arithmetic  10 us (4%)
    ppermute x32, waiting for transfers between devices, along_ring(): return lax.ppermute(array, 'dp', pairs)  52.7 us
    ppermute x32, starting transfers between devices, along_ring(): return lax.ppermute(array, 'dp', pairs)  32.7 us
    pallas_call x2, Pallas kernels, ffn_forward(): pl.pallas_call(functools.partial(ffn_forward_kernel, plan, ring.rows, chi...  20.7 us
    pallas_call x2, Pallas kernels, pair_grads(): pl.pallas_call(functools.partial(grad_kernel, chips, sources, cols), grid...  19.1 us
    pallas_call x2, Pallas kernels, ffn_backward(): pl.pallas_call(functools.partial(ffn_backward_kernel, plan, ring.rows, ch...  18 us
    ppermute x10, waiting for transfers between devices, swap_tensor(): lax.ppermute(array, 'tensor', [(i, i ^ bit) for i in range(self.tensor)])  14.7 us
    pallas_call x1, Pallas kernels, attend_backward(): pl.pallas_call(kernel, grid_spec=pltpu.PrefetchScalarGridSpec(num_scalar_...  13.9 us
    pallas_call x6, Pallas kernels, ring_add(): pl.pallas_call(ring_add_kernel, grid=(1,), in_specs=[pl.BlockSpec((1, row...  13.8 us
  transfers between devices with their start and end apart: 81, of which 36 were waited for; matrix products, arithmetic and copies ran while one was open for 5% of the time, Pallas kernels for 40%

commit v1 on v0

--- a/solution.py
+++ b/solution.py
@@ -300,7 +300,7 @@
 
 
 def grad_kernel(chips, sources, terms, me_ref, *refs):
-    scratch, out = refs[-1], refs[-2]
+    out, far_up, far_down, scratch = refs[-4:]
     d = 2 * pl.program_id(0)
     rows = out.shape[1]
     k = 0
@@ -321,6 +321,12 @@
             for i in range(2):
                 off = lanes * i + (chip_at(me_ref[0], d + i, chips) * rows) % lanes
                 out[i, :, cols] = scratch[pl.ds(pl.multiple_of(off, 32), rows), cols].astype(BF)
+
+    @pl.when(d == chips // 4 * 2)
+    def _():
+        block = out[chips // 2 % 2]
+        far_up[...] = block[: rows // 2]
+        far_down[...] = block[rows // 2 :]
 
 
 def pair_grads(me, chips, terms):
@@ -358,10 +364,12 @@
             num_scalar_prefetch=1,
             grid=(chips // 2,),
             in_specs=specs,
-            out_specs=pl.BlockSpec((2, rows, start), lambda d, m: (d, 0, 0)),
+            out_specs=[pl.BlockSpec((2, rows, start), lambda d, m: (d, 0, 0))]
+            + [pl.BlockSpec((rows // 2, start), lambda d, m: (0, 0))] * 2,
             scratch_shapes=[pltpu.VMEM((2 * lanes, start if lanes > rows else 128), F32)],
         ),
-        out_shape=jax.ShapeDtypeStruct((chips, rows, start), BF),
+        out_shape=[jax.ShapeDtypeStruct((chips, rows, start), BF)]
+        + [jax.ShapeDtypeStruct((rows // 2, start), BF)] * 2,
         compiler_params=PARAMS,
         cost_estimate=cost(flops, 8 << 20),
     )(me, *arrays)
@@ -904,12 +912,11 @@
 
 
 class Scatter:
-    def __init__(self, links, blocks):
+    def __init__(self, links, blocks, up, down):
         self.links, self.blocks, self.step = links, blocks, links.half_way
         self.arrived = None
         self.rows = blocks.shape[1]
-        far = blocks[self.step]
-        self.up, self.down = far[: self.rows // 2], far[self.rows // 2 :]
+        self.up, self.down = up, down
 
     def hops(self):
         for _ in range(max(1, self.links.half_way // 4)):
@@ -1109,9 +1116,9 @@
     terms[0][0] = (wide, *terms[0][0][1:])
     blocks = pair_grads(links.me, chips, terms)
     last = sums[parts - 1]
-    blocks, early, got = tie(blocks, early, last[1])
+    *blocks, early, got = tie(*blocks, early, last[1])
     sums[parts - 1] = (last[0], got)
-    ffn_sum = Scatter(links, blocks)
+    ffn_sum = Scatter(links, *blocks)
     ffn_sum.hops()
     for j in range(1, parts):
         first(j)
@@ -1137,8 +1144,8 @@
             (tokens_pair[0], pair, False, 0),
         ]
     blocks = pair_grads(links.me, chips, [qkv_terms, context_terms])
-    blocks, vector = ffn_sum.land(blocks, vector)
-    attn_sum = Scatter(links, blocks)
+    *blocks, vector = ffn_sum.land(*blocks, vector)
+    attn_sum = Scatter(links, *blocks)
     attn_sum.hops()
     ffn_sum.finish()
     vector = links.sum_far(vector)

time: 272 us -> 271 us (level)
  transfers between devices with their start and end apart: 81 -> 81, of which waited for: 36 -> 36; matrix products, arithmetic and copies ran while one was open for 5% -> 5% of each run, Pallas kernels for 40% -> 41%
where the time goes in v1:
time: 271 us; the launch traced here: 270 us
  Pallas kernels  114 us (42%)
  waiting for transfers between devices  72.6 us (27%)
  starting transfers between devices  56.2 us (21%)
  local copies, waits for them, and re-layouts  15.6 us (6%)
  other arithmetic  10 us (4%)
    ppermute x32, waiting for transfers between devices, along_ring(): return lax.ppermute(array, 'dp', pairs)  53 us
    ppermute x32, starting transfers between devices, along_ring(): return lax.ppermute(array, 'dp', pairs)  32.7 us
    pallas_call x2, Pallas kernels, ffn_forward(): pl.pallas_call(functools.partial(ffn_forward_kernel, plan, ring.rows, chi...  20.7 us
    pallas_call x2, Pallas kernels, pair_grads(): pl.pallas_call(functools.partial(grad_kernel, chips, sources, cols), grid...  19.4 us
    pallas_call x2, Pallas kernels, ffn_backward(): pl.pallas_call(functools.partial(ffn_backward_kernel, plan, ring.rows, ch...  18 us
    ppermute x10, waiting for transfers between devices, swap_tensor(): lax.ppermute(array, 'tensor', [(i, i ^ bit) for i in range(self.tensor)])  14.7 us
    pallas_call x1, Pallas kernels, attend_backward(): pl.pallas_call(kernel, grid_spec=pltpu.PrefetchScalarGridSpec(num_scalar_...  13.9 us
    pallas_call x6, Pallas kernels, ring_add(): pl.pallas_call(ring_add_kernel, grid=(1,), in_specs=[pl.BlockSpec((1, row...  13.8 us
  transfers between devices with their start and end apart: 81, of which 36 were waited for; matrix products, arithmetic and copies ran while one was open for 5% of the time, Pallas kernels for 41%

profile of v1, /device:TPU:0, one launch (start us, length us, event | category | flops | bytes accessed | tf_op | source)
XLA Modules:
  0.0 269.6 jit_solution(8346824974976953301)
XLA Ops:
  0.7 3.0 %collective-permute-start.2 = (bf16[1,256,1024]{2,1,0:T(8,128)(2,1)}, bf16[1,256,1024]{2,1,0:T(8,128)(2,1)S(1)}, u32[]{:S(2)}, u32[]{:S(2)}) collective-permute-start(bf16[1,256,1024]{2,1,0:T(8,128)(2,1)} %param.18), channel_id=1, source_target_pairs={{0,1},{1,0},{2,3},{3,2},{4,5},{5,4},{6,7},{7,6},{8,9},{9,8},{10,11... | collective-permute-start | bytes 1572872 | tf_op jit(solution)/shard_map/ppermute | solution.py:785
  10.1 3.2 %collective-permute-done.refs_4_ = bf16[64,2048]{1,0:T(8,128)(2,1)S(1)} collective-permute-done((bf16[64,2048]{1,0:T(8,128)(2,1)}, bf16[64,2048]{1,0:T(8,128)(2,1)S(1)}, u32[]{:S(2)}, u32[]{:S(2)}) %collective-permute-start) | collective-permute-done | bytes 262176 | tf_op jit(solution)/shard_map/ppermute | solution.py:793
  18.9 4.4 %collective-permute-done.3.refs_8_ = bf16[64,2048]{1,0:T(8,128)(2,1)S(1)} collective-permute-done((bf16[64,2048]{1,0:T(8,128)(2,1)S(1)}, bf16[64,2048]{1,0:T(8,128)(2,1)S(1)}, u32[]{:S(2)}, u32[]{:S(2)}) %collective-permute-start.3) | collective-permute-done | bytes 262176 | tf_op jit(solution)/shard_map/ppermute | solution.py:793
  27.1 3.8 %collective-permute-done.5.refs_12_ = bf16[64,2048]{1,0:T(8,128)(2,1)S(1)} collective-permute-done((bf16[64,2048]{1,0:T(8,128)(2,1)S(1)}, bf16[64,2048]{1,0:T(8,128)(2,1)S(1)}, u32[]{:S(2)}, u32[]{:S(2)}) %collective-permute-start.5) | collective-permute-done | bytes 262176 | tf_op jit(solution)/shard_map/ppermute | solution.py:793
  40.8 5.4 %collective-permute-done.9.refs_7_ = bf16[64,4096]{1,0:T(8,128)(2,1)S(1)} collective-permute-done((bf16[64,4096]{1,0:T(8,128)(2,1)S(1)}, bf16[64,4096]{1,0:T(8,128)(2,1)S(1)}, u32[]{:S(2)}, u32[]{:S(2)}) %collective-permute-start.9) | collective-permute-done | bytes 524320 | tf_op jit(solution)/shard_map/ppermute | solution.py:793
  53.3 7.0 %shard_map.306 = (bf16[1024,2048]{1,0:T(8,128)(2,1)}, bf16[512,1536]{1,0:T(8,128)(2,1)}) custom-call(s32[1]{0:T(128)} %bitcast.me_ref, f32[1,1536]{1,0:T(1,128)} %broadcast_in_dim_reshape.3.bias_ref, bf16[256,1024]{1,0:T(8,128)(2,1)} %bitcast.53, bf16[256,1024]{1,0:T(8,128)(2,1)} %bitcast.58, bf16[64,2048]{1,0:T(8,128)(2,1)} %shard_map.305.refs_2_, ...), custom_call_target="tpu_custom_call" | custom-call | flops 1572864 | bytes 16384 | tf_op jit(solution)/shard_map/pallas_call | solution.py:284
  60.4 8.8 %shard_map.307 = (bf16[512,512]{1,0:T(8,128)(2,1)}, f32[4,2,512]{2,1,0:T(2,128)}, bf16[256,1024]{1,0:T(8,128)(2,1)}, bf16[256,1024]{1,0:T(8,128)(2,1)}) custom-call(bf16[512,1536]{1,0:T(8,128)(2,1)} %get-tuple-element.151.qkv_ref, s32[1,1,512]{2,1,0:T(1,128)} %add_bitcast_fusion.row_ref, bf16[1024,2048]{1,0:T(8,128)(2,1)} %get-tuple-element.153.out_w_ref.w_ref), custom_call_target="tpu_custom_call" | custom-call | flops 3145728 | bytes 8192 | tf_op jit(solution)/shard_map/pallas_call | solution.py:79
  73.4 10.0 %collective-permute-done.25.refs_2_ = bf16[256,1024]{1,0:T(8,128)(2,1)S(1)} collective-permute-done((bf16[256,1024]{1,0:T(8,128)(2,1)}, bf16[256,1024]{1,0:T(8,128)(2,1)S(1)}, u32[]{:S(2)}, u32[]{:S(2)}) %collective-permute-start.25) | collective-permute-done | bytes 524320 | tf_op jit(solution)/shard_map/ppermute | solution.py:785
  89.3 5.6 %collective-permute-done.33.refs_17_ = bf16[32,4096]{1,0:T(8,128)(2,1)S(1)} collective-permute-done((bf16[32,4096]{1,0:T(8,128)(2,1)S(1)}, bf16[32,4096]{1,0:T(8,128)(2,1)S(1)}, u32[]{:S(2)}, u32[]{:S(2)}) %collective-permute-start.33) | collective-permute-done | bytes 262176 | tf_op jit(solution)/shard_map/ppermute | solution.py:793
  99.1 12.2 %shard_map.308 = (f32[256,1024]{1,0:T(8,128)}, bf16[256,1024]{1,0:T(8,128)(2,1)}, bf16[256,1024]{1,0:T(8,128)(2,1)}, bf16[256,1024]{1,0:T(8,128)(2,1)}, bf16[256...) custom-call(s32[1]{0:T(128)} %bitcast.me_ref, ...), custom_call_target="tpu_custom_call" | custom-call | flops 4194304 | bytes 16384 | tf_op jit(solution)/shard_map/pallas_call | solution.py:495
  112.7 8.5 %shard_map.309 = (f32[256,1024]{1,0:T(8,128)}, bf16[256,1024]{1,0:T(8,128)(2,1)}, bf16[256,1024]{1,0:T(8,128)(2,1)}, bf16[256,1024]{1,0:T(8,128)(2,1)}, bf16[256...) custom-call(s32[1]{0:T(128)} %bitcast.me_ref, f32[1,1024]{1,0:T(1,128)} %bitcast.82, ...), custom_call_target="tpu_custom_call" | custom-call | flops 4194304 | bytes 16384 | tf_op jit(solution)/shard_map/pallas_call | solution.py:495
  126.5 8.9 %shard_map.311 = (bf16[256,1024]{1,0:T(8,128)(2,1)}, f32[256,1024]{1,0:T(8,128)}, bf16[256,1024]{1,0:T(8,128)(2,1)}, bf16[256,1024]{1,0:T(8,128)(2,1)}, bf16[256...) custom-call(s32[1]{0:T(128)} %bitcast.me_ref, ...), custom_call_target="tpu_custom_call" | custom-call | flops 4194304 | bytes 16384 | tf_op jit(solution)/shard_map/pallas_call | solution.py:586
  138.1 9.0 %shard_map.310 = (bf16[256,1024]{1,0:T(8,128)(2,1)}, f32[256,1024]{1,0:T(8,128)}, bf16[256,1024]{1,0:T(8,128)(2,1)}, bf16[256,1024]{1,0:T(8,128)(2,1)}, bf16[256...) custom-call(s32[1]{0:T(128)} %bitcast.me_ref, ...), custom_call_target="tpu_custom_call" | custom-call | flops 4194304 | bytes 16384 | tf_op jit(solution)/shard_map/pallas_call | solution.py:586
  149.0 4.3 %shard_map.312 = (f32[256,1024]{1,0:T(8,128)}, bf16[256,1024]{1,0:T(8,128)(2,1)}, bf16[256,512]{1,0:T(8,128)(2,1)}, f32[3,1024]{1,0:T(4,128)}) custom-call(f32[256,1024]{1,0:T(8,128)} %get-tuple-element.172.mixed_ref, bf16[256,1024]{1,0:T(8,128)(2,1)} %get-tuple-element.180.own_ref, bf16[256,1024]{1,0:T(8,128)(2,1)} %collective-permute-done.41.got_ref, ...), custom_call_target="tpu_custom_call" | custom-call | flops 262144 | bytes 6144 | tf_op jit(solution)/shard_map/pallas_call | solution.py:638
  156.4 11.1 %shard_map.313 = (bf16[8,128,2048]{2,1,0:T(8,128)(2,1)}, bf16[64,2048]{1,0:T(8,128)(2,1)}, bf16[64,2048]{1,0:T(8,128)(2,1)}) custom-call(s32[1]{0:T(128)} %bitcast.me_ref, bf16[256,1024]{1,0:T(8,128)(2,1)} %get-tuple-element.184.refs_0_.refs_1_, bf16[256,1024]{1,0:T(8,128)(2,1)} %get-tuple-element.184.refs_0_.refs_1_, ...), custom_call_target="tpu_custom_call" | custom-call | flops 4194304 | bytes 8192 | tf_op jit(solution)/shard_map/pallas_call | solution.py:361
  169.7 4.3 %shard_map.314 = (f32[256,1024]{1,0:T(8,128)}, bf16[256,1024]{1,0:T(8,128)(2,1)}, bf16[256,512]{1,0:T(8,128)(2,1)}, f32[3,1024]{1,0:T(4,128)}) custom-call(f32[256,1024]{1,0:T(8,128)} %get-tuple-element.204.mixed_ref, bf16[256,1024]{1,0:T(8,128)(2,1)} %get-tuple-element.179.own_ref, bf16[256,1024]{1,0:T(8,128)(2,1)} %copy-done.38, ...), custom_call_target="tpu_custom_call" | custom-call | flops 262144 | bytes 6144 | tf_op jit(solution)/shard_map/pallas_call | solution.py:638
  178.1 2.5 shard_map.315
  183.2 13.9 %shard_map.316 = (bf16[512,1536]{1,0:T(8,128)(2,1)}, f32[1,1,1536]{2,1,0:T(1,128)}, f32[256,1024]{1,0:T(8,128)}, bf16[256,1024]{1,0:T(8,128)(2,1)}, bf16[512,768]{1,0:T(8,128)(2,1)}) custom-call(s32[1]{0:T(128)} %bitcast.me_ref, bf16[512,1536]{1,0:T(8,128)(2,1)} %get-tuple-element.151.qkv_ref, s32[1,1,512]{2,1,0:T(1,128)} %add_bitcast_fusion.row_ref, ...), custom_call_target="tpu_custom_call" | custom-call | flops 5242880 | bytes 8192 | tf_op jit(solution)/shard_map/pallas_call | solution.py:175
  200.2 2.6 shard_map.317
  206.8 8.3 %shard_map.318 = (bf16[8,128,1024]{2,1,0:T(8,128)(2,1)}, bf16[64,1024]{1,0:T(8,128)(2,1)}, bf16[64,1024]{1,0:T(8,128)(2,1)}) custom-call(s32[1]{0:T(128)} %bitcast.me_ref, bf16[256,1024]{1,0:T(8,128)(2,1)} %bitcast.55, bf16[256,1024]{1,0:T(8,128)(2,1)} %bitcast.56, bf16[512,1536]{1,0:T(8,128)(2,1)} %get-tuple-element.221.refs_2_.refs_5_, ...), custom_call_target="tpu_custom_call" | custom-call | flops 2097152 | bytes 8192 | tf_op jit(solution)/shard_map/pallas_call | solution.py:361
  221.3 2.5 collective-permute-start.71
  228.5 2.6 shard_map.323
  243.2 3.1 %collective-permute-done.78 = bf16[128,2048]{1,0:T(8,128)(2,1)} collective-permute-done((bf16[128,2048]{1,0:T(8,128)(2,1)}, bf16[128,2048]{1,0:T(8,128)(2,1)}, u32[]{:S(2)}, u32[]{:S(2)}) %collective-permute-start.78) | collective-permute-done | bytes 524320 | tf_op jit(solution)/shard_map/ppermute | solution.py:793
  257.8 6.1 %collective-permute-done.75 = bf16[128,1024]{1,0:T(8,128)(2,1)S(1)} collective-permute-done((bf16[128,1024]{1,0:T(8,128)(2,1)}, bf16[128,1024]{1,0:T(8,128)(2,1)S(1)}, u32[]{:S(2)}, u32[]{:S(2)}) %collective-permute-start.75) | collective-permute-done | bytes 262176 | tf_op jit(solution)/shard_map/ppermute | solution.py:793
  (345 shorter events, 116.8 us)
Async XLA Ops:
  0.7 15.1 %collective-permute-start.2 = (bf16[1,256,1024]{2,1,0:T(8,128)(2,1)}, bf16[1,256,1024]{2,1,0:T(8,128)(2,1)S(1)}, u32[]{:S(2)}, u32[]{:S(2)}) collective-permute-start(bf16[1,256,1024]{2,1,0:T(8,128)(2,1)} %param.18), channel_id=1, source_target_pairs={{0,1},{1,0},{2,3},{3,2},{4,5},{5,4},{6,7},{7,6},{8,9},{9,8},{10,11... | collective-permute-start | bytes 1572872 | tf_op jit(solution)/shard_map/ppermute | solution.py:785
  39.3 29.8 %collective-permute-start.24 = (bf16[1,256,1024]{2,1,0:T(8,128)(2,1)}, bf16[1,256,1024]{2,1,0:T(8,128)(2,1)S(1)}, u32[]{:S(2)}, u32[]{:S(2)}) collective-permute-start(bf16[1,256,1024]{2,1,0:T(8,128)(2,1)} %param.35), channel_id=1, source_target_pairs={{0,1},{1,0},{2,3},{3,2},{4,5},{5,4},{6,7},{7,6},{8,9},{9,8},{10,11... | collective-permute-start | bytes 1572872 | tf_op jit(solution)/shard_map/ppermute | solution.py:785
  46.2 24.6 %collective-permute-start.10 = (bf16[64,4096]{1,0:T(8,128)(2,1)S(1)}, bf16[64,4096]{1,0:T(8,128)(2,1)}, u32[]{:S(2)}, u32[]{:S(2)}) collective-permute-start(bf16[64,4096]{1,0:T(8,128)(2,1)S(1)} %collective-permute-done.9.refs_7_), channel_id=1, source_target_pairs={{0,4},{2,6},{8,0},{10,2},{16,8},{18,10},{24,16},{26,18},{28,24},{3... | collective-permute-start | bytes 1572872 | tf_op jit(solution)/shard_map/ppermute | solution.py:793
  46.7 24.2 %collective-permute-start.8 = (bf16[64,4096]{1,0:T(8,128)(2,1)S(1)}, bf16[64,4096]{1,0:T(8,128)(2,1)}, u32[]{:S(2)}, u32[]{:S(2)}) collective-permute-start(bf16[64,4096]{1,0:T(8,128)(2,1)S(1)} %collective-permute-done.7.refs_5_), channel_id=1, source_target_pairs={{0,8},{2,10},{8,16},{10,18},{16,24},{18,26},{24,28},{26,30},{28,20... | collective-permute-start | bytes 1572872 | tf_op jit(solution)/shard_map/ppermute | solution.py:793
  69.1 14.3 %collective-permute-start.25 = (bf16[256,1024]{1,0:T(8,128)(2,1)}, bf16[256,1024]{1,0:T(8,128)(2,1)S(1)}, u32[]{:S(2)}, u32[]{:S(2)}) collective-permute-start(bf16[256,1024]{1,0:T(8,128)(2,1)} %get-tuple-element.160.refs_1_), channel_id=1, source_target_pairs={{0,1},{1,0},{2,3},{3,2},{4,5},{5,4},{6,7},{7,6},{8,9},{9,8},{10,11... | collective-permute-start | bytes 1572872 | tf_op jit(solution)/shard_map/ppermute | solution.py:785
  70.9 13.9 %collective-permute-start.22 = (bf16[64,4096]{1,0:T(8,128)(2,1)}, bf16[64,4096]{1,0:T(8,128)(2,1)S(1)}, u32[]{:S(2)}, u32[]{:S(2)}) collective-permute-start(bf16[64,4096]{1,0:T(8,128)(2,1)} %collective-permute-done.8.refs_9_), channel_id=1, source_target_pairs={{0,8},{2,10},{8,16},{10,18},{16,24},{18,26},{24,28},{26,30},{28,20... | collective-permute-start | bytes 1572872 | tf_op jit(solution)/shard_map/ppermute | solution.py:793
  72.9 15.1 %collective-permute-start.27 = (bf16[64,4096]{1,0:T(8,128)(2,1)S(1)}, bf16[64,4096]{1,0:T(8,128)(2,1)S(1)}, u32[]{:S(2)}, u32[]{:S(2)}) collective-permute-start(bf16[64,4096]{1,0:T(8,128)(2,1)S(1)} %collective-permute-done.7.refs_5_), channel_id=1, source_target_pairs={{0,2},{2,0},{4,6},{6,4},{8,10},{10,8},{12,14},{14,12},{16,18},{18,... | collective-permute-start | bytes 1572872 | tf_op jit(solution)/shard_map/ppermute | solution.py:782
  88.8 23.1 %collective-permute-start.37 = (bf16[256,1024]{1,0:T(8,128)(2,1)}, bf16[256,1024]{1,0:T(8,128)(2,1)S(1)}, u32[]{:S(2)}, u32[]{:S(2)}) collective-permute-start(bf16[256,1024]{1,0:T(8,128)(2,1)} %get-tuple-element.155.refs_1_), channel_id=1, source_target_pairs={{0,1},{1,0},{2,3},{3,2},{4,5},{5,4},{6,7},{7,6},{8,9},{9,8},{10,11... | collective-permute-start | bytes 1572872 | tf_op jit(solution)/shard_map/ppermute | solution.py:785
  111.3 15.1 %collective-permute-start.39 = (bf16[256,1024]{1,0:T(8,128)(2,1)}, bf16[256,1024]{1,0:T(8,128)(2,1)}, u32[]{:S(2)}, u32[]{:S(2)}) collective-permute-start(bf16[256,1024]{1,0:T(8,128)(2,1)} %get-tuple-element.165.refs_1_), channel_id=1, source_target_pairs={{0,1},{1,0},{2,3},{3,2},{4,5},{5,4},{6,7},{7,6},{8,9},{9,8},{10,11... | collective-permute-start | bytes 1572872 | tf_op jit(solution)/shard_map/ppermute | solution.py:785
  121.2 15.6 %collective-permute-start.38 = (bf16[256,1024]{1,0:T(8,128)(2,1)}, bf16[256,1024]{1,0:T(8,128)(2,1)S(1)}, u32[]{:S(2)}, u32[]{:S(2)}) collective-permute-start(bf16[256,1024]{1,0:T(8,128)(2,1)} %get-tuple-element.168.refs_1_), channel_id=1, source_target_pairs={{0,1},{1,0},{2,3},{3,2},{4,5},{5,4},{6,7},{7,6},{8,9},{9,8},{10,11... | collective-permute-start | bytes 1572872 | tf_op jit(solution)/shard_map/ppermute | solution.py:785
  122.9 14.8 %collective-permute-start.45 = (bf16[256,1024]{1,0:T(8,128)(2,1)}, bf16[256,1024]{1,0:T(8,128)(2,1)S(1)}, u32[]{:S(2)}, u32[]{:S(2)}) collective-permute-start(bf16[256,1024]{1,0:T(8,128)(2,1)} %get-tuple-element.189), channel_id=1, source_target_pairs={{0,2},{2,0},{4,6},{6,4},{8,10},{10,8},{12,14},{14,12},{16,18},{18,... | collective-permute-start | bytes 1572872 | tf_op jit(solution)/shard_map/ppermute | solution.py:782
  124.1 23.2 %collective-permute-start.48 = (bf16[256,1024]{1,0:T(8,128)(2,1)}, bf16[256,1024]{1,0:T(8,128)(2,1)S(1)}, u32[]{:S(2)}, u32[]{:S(2)}) collective-permute-start(bf16[256,1024]{1,0:T(8,128)(2,1)} %get-tuple-element.192.refs_15_.refs_16_), channel_id=1, source_target_pairs={{0,2},{2,0},{4,6},{6,4},{8,10},{10,8},{12,14},{14,12},{16,18},{18,... | collective-permute-start | bytes 1572872 | tf_op jit(solution)/shard_map/ppermute | solution.py:782
  124.4 23.0 %collective-permute-start.43 = (bf16[256,1024]{1,0:T(8,128)(2,1)}, bf16[256,1024]{1,0:T(8,128)(2,1)S(1)}, u32[]{:S(2)}, u32[]{:S(2)}) collective-permute-start(bf16[256,1024]{1,0:T(8,128)(2,1)} %get-tuple-element.188), channel_id=1, source_target_pairs={{0,2},{2,0},{4,6},{6,4},{8,10},{10,8},{12,14},{14,12},{16,18},{18,... | collective-permute-start | bytes 1572872 | tf_op jit(solution)/shard_map/ppermute | solution.py:782
  137.6 16.4 %collective-permute-start.44 = (bf16[256,1024]{1,0:T(8,128)(2,1)}, bf16[256,1024]{1,0:T(8,128)(2,1)S(1)}, u32[]{:S(2)}, u32[]{:S(2)}) collective-permute-start(bf16[256,1024]{1,0:T(8,128)(2,1)} %get-tuple-element.186.refs_3_.refs_4_), channel_id=1, source_target_pairs={{0,2},{2,0},{4,6},{6,4},{8,10},{10,8},{12,14},{14,12},{16,18},{18,... | collective-permute-start | bytes 1572872 | tf_op jit(solution)/shard_map/ppermute | solution.py:782
  148.4 19.2 %collective-permute-start.51 = (bf16[256,1024]{1,0:T(8,128)(2,1)}, bf16[256,1024]{1,0:T(8,128)(2,1)S(1)}, u32[]{:S(2)}, u32[]{:S(2)}) collective-permute-start(bf16[256,1024]{1,0:T(8,128)(2,1)} %get-tuple-element.180.own_ref), channel_id=1, source_target_pairs={{0,1},{1,0},{2,3},{3,2},{4,5},{5,4},{6,7},{7,6},{8,9},{9,8},{10,11... | collective-permute-start | bytes 1572872 | tf_op jit(solution)/shard_map/ppermute | solution.py:785
  180.7 17.2 %collective-permute-start.54 = (bf16[128,2048]{1,0:T(8,128)(2,1)}, bf16[128,2048]{1,0:T(8,128)(2,1)S(1)}, u32[]{:S(2)}, u32[]{:S(2)}) collective-permute-start(bf16[128,2048]{1,0:T(8,128)(2,1)} %get-tuple-element.210), channel_id=1, source_target_pairs={{0,8},{2,10},{8,16},{10,18},{16,24},{18,26},{24,28},{26,30},{28,20... | collective-permute-start | bytes 1572872 | tf_op jit(solution)/shard_map/ppermute | solution.py:793
  181.3 16.6 %collective-permute-start.55 = (bf16[128,2048]{1,0:T(8,128)(2,1)}, bf16[128,2048]{1,0:T(8,128)(2,1)}, u32[]{:S(2)}, u32[]{:S(2)}) collective-permute-start(bf16[128,2048]{1,0:T(8,128)(2,1)} %get-tuple-element.211), channel_id=1, source_target_pairs={{0,4},{2,6},{8,0},{10,2},{16,8},{18,10},{24,16},{26,18},{28,24},{3... | collective-permute-start | bytes 1572872 | tf_op jit(solution)/shard_map/ppermute | solution.py:793
  182.7 16.9 %collective-permute-start.58 = (bf16[256,1024]{1,0:T(8,128)(2,1)S(1)}, bf16[256,1024]{1,0:T(8,128)(2,1)S(1)}, u32[]{:S(2)}, u32[]{:S(2)}) collective-permute-start(bf16[256,1024]{1,0:T(8,128)(2,1)S(1)} %bitcast.57), channel_id=1, source_target_pairs={{0,2},{2,0},{4,6},{6,4},{8,10},{10,8},{12,14},{14,12},{16,18},{18,... | collective-permute-start | bytes 1572872 | tf_op jit(solution)/shard_map/ppermute | solution.py:782
  182.7 20.1 %collective-permute-start.60 = (bf16[256,1024]{1,0:T(8,128)(2,1)S(1)}, bf16[256,1024]{1,0:T(8,128)(2,1)}, u32[]{:S(2)}, u32[]{:S(2)}) collective-permute-start(bf16[256,1024]{1,0:T(8,128)(2,1)S(1)} %bitcast.62), channel_id=1, source_target_pairs={{0,2},{2,0},{4,6},{6,4},{8,10},{10,8},{12,14},{14,12},{16,18},{18,... | collective-permute-start | bytes 1572872 | tf_op jit(solution)/shard_map/ppermute | solution.py:782
  202.8 14.2 %collective-permute-start.56 = (bf16[128,2048]{1,0:T(8,128)(2,1)}, bf16[128,2048]{1,0:T(8,128)(2,1)S(1)}, u32[]{:S(2)}, u32[]{:S(2)}) collective-permute-start(bf16[128,2048]{1,0:T(8,128)(2,1)} %get-tuple-element.219), channel_id=1, source_target_pairs={{0,8},{2,10},{8,16},{10,18},{16,24},{18,26},{24,28},{26,30},{28,20... | collective-permute-start | bytes 1572872 | tf_op jit(solution)/shard_map/ppermute | solution.py:793
  203.3 14.1 %collective-permute-start.57 = (bf16[128,2048]{1,0:T(8,128)(2,1)}, bf16[128,2048]{1,0:T(8,128)(2,1)S(1)}, u32[]{:S(2)}, u32[]{:S(2)}) collective-permute-start(bf16[128,2048]{1,0:T(8,128)(2,1)} %get-tuple-element.220), channel_id=1, source_target_pairs={{0,4},{2,6},{8,0},{10,2},{16,8},{18,10},{24,16},{26,18},{28,24},{3... | collective-permute-start | bytes 1572872 | tf_op jit(solution)/shard_map/ppermute | solution.py:793
  231.1 15.2 %collective-permute-start.78 = (bf16[128,2048]{1,0:T(8,128)(2,1)}, bf16[128,2048]{1,0:T(8,128)(2,1)}, u32[]{:S(2)}, u32[]{:S(2)}) collective-permute-start(bf16[128,2048]{1,0:T(8,128)(2,1)} %get-tuple-element.260), channel_id=1, source_target_pairs={{0,8},{2,10},{8,16},{10,18},{16,24},{18,26},{24,28},{26,30},{28,20... | collective-permute-start | bytes 1572872 | tf_op jit(solution)/shard_map/ppermute | solution.py:793
  232.6 15.7 %collective-permute-start.79 = (bf16[128,2048]{1,0:T(8,128)(2,1)}, bf16[128,2048]{1,0:T(8,128)(2,1)}, u32[]{:S(2)}, u32[]{:S(2)}) collective-permute-start(bf16[128,2048]{1,0:T(8,128)(2,1)} %get-tuple-element.261), channel_id=1, source_target_pairs={{0,4},{2,6},{8,0},{10,2},{16,8},{18,10},{24,16},{26,18},{28,24},{3... | collective-permute-start | bytes 1572872 | tf_op jit(solution)/shard_map/ppermute | solution.py:793
  233.2 16.8 %collective-permute-start.74 = (bf16[256,1024]{1,0:T(8,128)(2,1)}, bf16[256,1024]{1,0:T(8,128)(2,1)}, u32[]{:S(2)}, u32[]{:S(2)}) collective-permute-start(bf16[256,1024]{1,0:T(8,128)(2,1)} %get-tuple-element.248), channel_id=1, source_target_pairs={{0,1},{1,0},{2,3},{3,2},{4,5},{5,4},{6,7},{7,6},{8,9},{9,8},{10,11... | collective-permute-start | bytes 1572872 | tf_op jit(solution)/shard_map/ppermute | solution.py:785
  (133 other events, 1184.1 us)
